TPU v7x, 256 devices: a whole 4x4x8 slice. The times are simulated.
256 devices in a mesh: patch: 64 (over z, y, core), sample: 4 (over x).
Axes of the slice: x: 4, y: 4, z: 8, core: 2. Of those that a mesh axis runs over, the one named last changes fastest.
Arguments:
- features: bfloat16 [4, 32768, 512], P('sample', 'patch'), may hold values from -600 to 600
- cotangent: bfloat16 [4, 32768, 512], P('sample', 'patch'), may hold values from -6 to 6
- weight_qkv: bfloat16 [512, 1536], replicated, may hold values from -5 to 5
- weight_out: bfloat16 [512, 512], replicated, may hold values from -0.25 to 0.25
- key_tiles: int32 [256, 8], replicated, may hold values from 0 to 255, as said below
- tile_valid: int32 [256, 8], replicated, may hold values from 0 to 1, as said below
Outputs:
- grad_features: bfloat16 [4, 32768, 512], P('sample', 'patch')
- grad_qkv: float32 [512, 1536], replicated
- grad_out: float32 [512, 512], replicated
Inputs may be any that keep to these rules, and one draw needn't show every extreme that they name: `key_tiles`: row g names 8 distinct tile ids. A tile's patch is its id // 4. The first id is g itself, the next 3 are other tiles of g's patch, and the last 4 lie one each in the patches at offsets -2 to 2 other than 0 around the cycle of patches, in rising order of offset. Over the rows of one patch exactly 2 distinct tiles of each such neighbouring patch are named. `tile_valid`: column 0 is always 1.
All inputs are finite; a program needn't handle non-finite values.
Results may differ from a plain program's by a relative error of at most 0.0088.
Values may be sent and summed in bfloat16 or wider, within the bound.
A program may use at most 192 MiB of HBM per device.

v0:
```python
from functools import partial
import math

import jax
import jax.numpy as jnp
from jax import lax
from jax.sharding import PartitionSpec as P

HEADS = 4
TILE = 128
NB = 8
REACH = 2


epsilon = 1e-06


def from_behind(value, axis, steps):
    count = lax.axis_size(axis)
    pairs = [(source, (source + steps) % count) for source in range(count)]
    return lax.ppermute(value, axis, pairs)


def tile_backward(query_tile, pair_tiles, live_flags, grad_tile, head_count):
    row_count = query_tile.shape[0]
    model_width = query_tile.shape[1]
    head_width = model_width // head_count
    scaling = head_width ** (-0.5)
    key_heads = pair_tiles[:, :, :model_width].reshape(-1, head_count, head_width)
    value_heads = pair_tiles[:, :, model_width:].reshape(-1, head_count, head_width)
    query_heads = query_tile.reshape(row_count, head_count, head_width)
    grad_heads = grad_tile.reshape(row_count, head_count, head_width)
    scores = (
        jnp.einsum("qhd,khd->hqk", query_heads, key_heads, preferred_element_type=jnp.float32)
        * scaling
    )
    live_mask = jnp.repeat(live_flags > 0, pair_tiles.shape[1])
    scores = jnp.where(live_mask[None, None, :], scores, -jnp.inf)
    highest = jnp.max(scores, -1, keepdims=True)
    expanded = jnp.exp(scores - highest)
    attention = expanded / jnp.sum(expanded, -1, keepdims=True)
    attention_low = attention.astype(jnp.bfloat16)
    attended = jnp.einsum(
        "hqk,khd->qhd", attention_low, value_heads, preferred_element_type=jnp.float32
    )
    attended = attended.astype(jnp.bfloat16).reshape(row_count, model_width)
    dprob = jnp.einsum("qhd,khd->hqk", grad_heads, value_heads, preferred_element_type=jnp.float32)
    centre = jnp.sum(attention * dprob, -1, keepdims=True)
    dscore = (attention * (dprob - centre) * scaling).astype(jnp.bfloat16)
    dquery = jnp.einsum(
        "hqk,khd->qhd", dscore, key_heads, preferred_element_type=jnp.float32
    ).reshape(row_count, model_width)
    dkey = jnp.einsum("hqk,qhd->khd", dscore, query_heads, preferred_element_type=jnp.float32)
    dvalue = jnp.einsum(
        "hqk,qhd->khd", attention_low, grad_heads, preferred_element_type=jnp.float32
    )
    dkey = dkey.reshape(pair_tiles.shape[0], pair_tiles.shape[1], model_width)
    dvalue = dvalue.reshape(pair_tiles.shape[0], pair_tiles.shape[1], model_width)
    return (attended, dquery, jnp.concatenate([dkey, dvalue], -1))


def on_device(features, cotangent, weight_qkv, weight_out, key_tiles, tile_valid):
    patches = lax.axis_size("patch")
    position = lax.axis_index("patch")
    rows_local = features.shape[1]
    model_width = features.shape[2]
    tile_count = rows_local // TILE
    offsets = [shift_by for shift_by in range(-REACH, REACH + 1) if shift_by != 0]
    inputs = features[0].astype(jnp.float32)
    inverse = lax.rsqrt(jnp.mean(inputs * inputs, -1, keepdims=True) + epsilon)
    normed = inputs * inverse
    normed_low = normed.astype(jnp.bfloat16)
    projected = jnp.dot(normed_low, weight_qkv, preferred_element_type=jnp.float32).astype(
        jnp.bfloat16
    )
    queries = projected[:, :model_width]
    pairs_own = projected[:, model_width:].reshape(tile_count, TILE, 2 * model_width)
    grad_rows = cotangent[0]
    grad_attended = jnp.einsum(
        "pe,de->pd", grad_rows, weight_out, preferred_element_type=jnp.float32
    ).astype(jnp.bfloat16)
    my_lists = lax.dynamic_slice_in_dim(key_tiles, position * tile_count, tile_count, 0)
    my_valid = lax.dynamic_slice_in_dim(tile_valid, position * tile_count, tile_count, 0)
    owner_patch = my_lists // tile_count
    within = my_lists % tile_count
    distance = (owner_patch - position) % patches
    distance = jnp.where(distance > patches // 2, distance - patches, distance)
    order_index = jnp.where(distance < 0, distance + REACH, distance + REACH - 1)
    arrivals = []
    for shift_by in offsets:
        arrivals.append(from_behind(pairs_own, "patch", -shift_by))
    buffer = jnp.concatenate([pairs_own] + arrivals, 0)
    slot_ids = jnp.where(distance == 0, within, tile_count + order_index * tile_count + within)
    group_size = math.gcd(4, tile_count)
    step_count = tile_count // group_size
    tile_pass = jax.vmap(partial(tile_backward, head_count=HEADS))
    buffer_count = buffer.shape[0]

    def advance(running, pieces):
        query_group, slot_group, live_group, grad_group = pieces
        flat_slots = slot_group.reshape(-1)
        gathered = jnp.take(buffer, flat_slots, axis=0).reshape(
            group_size, NB, TILE, 2 * model_width
        )
        attended, dquery, dpairs = tile_pass(query_group, gathered, live_group, grad_group)
        running = running.at[flat_slots].add(dpairs.reshape(group_size * NB, TILE, 2 * model_width))
        return (running, (attended, dquery))

    start_sums = jnp.zeros((buffer_count, TILE, 2 * model_width), jnp.float32)
    scanned = (
        queries.reshape(step_count, group_size, TILE, model_width),
        slot_ids.reshape(step_count, group_size, NB),
        my_valid.reshape(step_count, group_size, NB),
        grad_attended.reshape(step_count, group_size, TILE, model_width),
    )
    totals, (attended_all, dquery_all) = lax.scan(advance, start_sums, scanned)
    grads_own = totals[:tile_count]
    for offset_index, shift_by in enumerate(offsets):
        portion = totals[
            tile_count + offset_index * tile_count : tile_count + (offset_index + 1) * tile_count
        ]
        grads_own = grads_own + from_behind(portion.astype(jnp.bfloat16), "patch", shift_by).astype(
            portion.dtype
        )
    attended_rows = attended_all.reshape(rows_local, model_width)
    grad_projected = jnp.concatenate(
        [
            dquery_all.reshape(rows_local, model_width),
            grads_own.reshape(rows_local, 2 * model_width),
        ],
        1,
    ).astype(jnp.bfloat16)
    grad_normed = jnp.einsum(
        "pe,de->pd", grad_projected, weight_qkv, preferred_element_type=jnp.float32
    )
    grad_inputs = grad_rows.astype(jnp.float32) + inverse * (
        grad_normed - normed * jnp.mean(grad_normed * normed, -1, keepdims=True)
    )
    local_qkv = jnp.einsum(
        "pd,pe->de", normed_low, grad_projected, preferred_element_type=jnp.float32
    )
    local_out = jnp.einsum(
        "pd,pe->de", attended_rows, grad_rows, preferred_element_type=jnp.float32
    )
    summed_qkv, summed_out = lax.psum((local_qkv, local_out), ("patch", "sample"))
    factor = float(lax.axis_size("patch") * lax.axis_size("sample") * rows_local) ** (-0.5)
    return (grad_inputs.astype(jnp.bfloat16)[None], summed_qkv * factor, summed_out * factor)


def solution(mesh):
    placed = (P("sample", "patch", None), P("sample", "patch", None), P(), P(), P(), P())
    return jax.shard_map(
        on_device,
        mesh=mesh,
        in_specs=placed,
        out_specs=(P("sample", "patch", None), P(), P()),
        check_vma=False,
    )
```

profile of v0, /device:TPU:1, one launch (start us, length us, event | category | flops | bytes accessed | tf_op | source)
XLA Modules:
  0.0 586.8 jit_solution(10732911310257279190)
XLA Ops:
  7.2 1.4 copy.38
  9.8 1.1 copy-done.5
  11.0 1.1 slice.44
  12.1 2.1 collective-permute-start
  14.2 2.1 collective-permute-start.1
  16.3 5.3 collective-permute-start.3
  24.1 2.0 copy.49
  26.2 1.5 convolution_convert_fusion.1
  28.6 1.3 copy.51
  30.0 2.3 constant_dynamic-update-slice_fusion.4
  32.2 11.9 %collective-permute-done = bf16[4,128,1024]{2,1,0:T(8,128)(2,1)} collective-permute-done((bf16[4,128,1024]{2,1,0:T(8,128)(2,1)}, bf16[4,128,1024]{2,1,0:T(8,128)(2,1)}, u32[]{:S(2)}, u32[]{:S(2)}) %collective-permute-start) | collective-permute-done | bytes 1048608 | tf_op jit(solution)/shard_map/ppermute | solution.py:21
  44.1 2.3 constant_dynamic-update-slice_fusion.3
  46.4 2.3 collective-permute-done.1
  48.7 2.3 constant_dynamic-update-slice_fusion.2
  51.0 2.3 constant_dynamic-update-slice_fusion.1
  53.3 2.3 constant_dynamic-update-slice_fusion
  55.5 7.6 %gather_fusion = bf16[32,128,1024]{2,1,0:T(8,128)(2,1)} fusion(bf16[20,128,1024]{2,1,0:T(8,128)(2,1)} %constant_dynamic-update-slice_fusion, s32[1024]{0:T(1024)S(1)} %pad_clamp_fusion), kind=kCustom, calls=%fused_computation | custom fusion | bytes 16777344 | tf_op jit(solution)/shard_map/while/body/eval_jaxpr/jit(_take)/gather | solution.py:102
  63.1 7.5 %broadcast_select_fusion = bf16[4,8,128,1024]{3,2,1,0:T(8,128)(2,1)} fusion(bf16[4,8,128,1024]{3,2,1,0:T(8,128)(2,1)} %bitcast.63, pred[4,8]{1,0:T(4,128)(4,1)S(1)} %copy.39), kind=kLoop, calls=%fused_computation.10 | loop fusion | flops 4194304 | bytes 16777248 | tf_op jit(solution)/shard_map/while/body/eval_jaxpr/jit(_take)/select_n | solution.py:102
  70.6 5.9 fusion.70
  76.5 6.9 %reshape.155 = bf16[4,1024,4,128]{3,2,1,0:T(4,128)(2,1)} reshape(bf16[4,8,128,512]{3,2,1,0:T(8,128)(2,1)} %get-tuple-element.44) | data formatting | bytes 8388608 | tf_op jit(solution)/shard_map/while/body/eval_jaxpr/vmap()/reshape | solution.py:29
  83.4 7.6 %copy.57 = bf16[4,1024,4,128]{1,3,2,0:T(8,128)(2,1)} copy(bf16[4,1024,4,128]{3,2,1,0:T(4,128)(2,1)} %reshape.155) | data formatting | bytes 8388608 | tf_op jit(solution)/shard_map/while/body/eval_jaxpr/vmap()/reshape | solution.py:29
  90.9 6.9 %reshape.156 = bf16[4,1024,4,128]{3,2,1,0:T(4,128)(2,1)} reshape(bf16[4,8,128,512]{3,2,1,0:T(8,128)(2,1)} %get-tuple-element.43) | data formatting | bytes 8388608 | tf_op jit(solution)/shard_map/while/body/eval_jaxpr/vmap()/reshape | solution.py:30
  97.8 7.5 %copy.56 = bf16[4,1024,4,128]{1,3,2,0:T(8,128)(2,1)} copy(bf16[4,1024,4,128]{3,2,1,0:T(4,128)(2,1)} %reshape.156) | data formatting | bytes 8388608 | tf_op jit(solution)/shard_map/while/body/eval_jaxpr/vmap()/reshape | solution.py:30
  105.3 6.7 %fusion.73 = f32[4,4,128,1024]{3,2,1,0:T(8,128)} fusion(bf16[4,128,4,128]{1,3,2,0:T(8,128)(2,1)S(1)} %copy.51, bf16[4,1024,4,128]{1,3,2,0:T(8,128)(2,1)} %copy.56), kind=kOutput, calls=%fused_computation.98 | convolution fusion | flops 536870912 | bytes 13107200 | tf_op jit(solution)/shard_map/while/body/eval_jaxpr/vmap(qhd,khd->hqk)/dot_general | solution.py:47
  112.0 8.8 %fusion.72 = (f32[4,4,128]{2,1,0:T(4,128)S(1)}, f32[4,4,128,1024]{3,2,1,0:T(8,128)}) fusion(pred[4,1024]{1,0:T(4,128)(4,1)S(1)} %bitcast.70, bf16[4,128,4,128]{1,3,2,0:T(8,128)(2,1)} %copy.49, bf16[4,1024,4,128]{1,3,2,0:T(8,128)(2,1)} %copy.57), kind=kOutput, calls=%fused_computation.97 | convolution fusion | flops 545260544 | bytes 13119488 | tf_op jit(solution)/shard_map/while/body/eval_jaxpr/vmap()/sub | solution.py:40
  120.8 7.9 %convolution_bitcast_fusion = f32[4,1024,4,128]{1,3,2,0:T(8,128)} fusion(bf16[4,128,4,128]{1,3,2,0:T(8,128)(2,1)S(1)} %copy.51, f32[4,4,128,1024]{3,2,1,0:T(8,128)} %get-tuple-element.50, f32[4,4,128]{2,1,0:T(4,128)S(1)} %get-tuple-element.49), kind=kOutput, calls=%fused_computation.19 | convolution fusion | flops 541065216 | bytes 17309696 | tf_op jit(solution)/shard_map/while/body/eval_jaxpr/vmap(hqk,qhd->khd)/dot_general | solution.py:54
  128.8 24.0 %fusion.15 = f32[4,1024,4,128]{1,3,2,0:T(8,128)} fusion(bf16[4,128,4,128]{1,3,2,0:T(8,128)(2,1)} %copy.49, f32[4,4,128,1024]{3,2,1,0:T(8,128)} %fusion.73, f32[4,4,128,1024]{3,2,1,0:T(8,128)} %get-tuple-element.50, f32[4,4,128]{2,1,0:T(4,128)S(1)} %get-tuple-element.49), kind=kOutput, calls=%fused_computation.18 | convolution fusion | flops 551554048 | bytes 25698304 | tf_op jit(solution)/shard_map/while/body/eval_jaxpr/vmap(hqk,qhd->khd)/dot_general | solution.py:53
  152.7 9.9 %copy.50 = f32[4,1024,4,128]{3,2,1,0:T(4,128)} copy(f32[4,1024,4,128]{1,3,2,0:T(8,128)} %fusion.15) | data formatting | bytes 16777216 | tf_op jit(solution)/shard_map/while/body/eval_jaxpr/vmap(hqk,qhd->khd)/transpose | solution.py:53
  162.6 10.3 %concatenate.17 = f32[32,128,512]{2,1,0:T(8,128)} reshape(f32[4,1024,4,128]{3,2,1,0:T(4,128)} %copy.50) | data formatting | bytes 16777216 | tf_op jit(solution)/shard_map/while/body/eval_jaxpr/vmap()/concatenate | solution.py:59
  172.9 9.9 %copy.52 = f32[4,1024,4,128]{3,2,1,0:T(4,128)} copy(f32[4,1024,4,128]{1,3,2,0:T(8,128)} %convolution_bitcast_fusion) | data formatting | bytes 16777216 | tf_op jit(solution)/shard_map/while/body/eval_jaxpr/vmap(hqk,qhd->khd)/transpose | solution.py:54
  182.8 10.3 %concatenate.18 = f32[32,128,512]{2,1,0:T(8,128)} reshape(f32[4,1024,4,128]{3,2,1,0:T(4,128)} %copy.52) | data formatting | bytes 16777216 | tf_op jit(solution)/shard_map/while/body/eval_jaxpr/vmap()/concatenate | solution.py:59
  193.0 11.7 %pad_maximum_fusion = f32[32,128,1024]{2,1,0:T(8,128)} fusion(f32[32,128,512]{2,1,0:T(8,128)} %concatenate.18, f32[32,128,512]{2,1,0:T(8,128)} %concatenate.17), kind=kLoop, calls=%fused_computation.4 | loop fusion | flops 4194304 | bytes 33554432 | tf_op jit(solution)/shard_map/while/body/eval_jaxpr/vmap()/concatenate | solution.py:59
  204.8 5.2 broadcast_in_dim.64
  210.0 36.2 %scatter_fusion = f32[20,128,1024]{2,1,0:T(8,128)} fusion(f32[20,128,1024]{2,1,0:T(8,128)} %broadcast_in_dim.64, s32[32]{0:T(128)S(1)} %fusion.61, f32[32,128,1024]{2,1,0:T(8,128)} %pad_maximum_fusion), kind=kCustom, calls=%fused_computation.1 | custom fusion | flops 4194304 | bytes 50331776 | tf_op jit(solution)/shard_map/while/body/eval_jaxpr/scatter-add | solution.py:106
  246.1 4.8 convert.17
  251.0 2.3 fusion.71
  253.3 6.8 %collective-permute-start.4 = (bf16[4,128,1024]{2,1,0:T(8,128)(2,1)}, bf16[4,128,1024]{2,1,0:T(8,128)(2,1)}, u32[]{:S(2)}, u32[]{:S(2)}) collective-permute-start(bf16[4,128,1024]{2,1,0:T(8,128)(2,1)} %get-tuple-element.45), channel_id=1, source_target_pairs={{0,248},{4,252},{8,0},{12,4},{16,8},{20,12},{24,16},{28,20},{32,24... | collective-permute-start | bytes 3145736 | tf_op jit(solution)/shard_map/ppermute | solution.py:21
  260.1 2.7 collective-permute-start.5
  263.0 4.7 fusion.34
  268.8 22.9 %fusion.37 = bf16[4,128,4,128]{1,3,2,0:T(8,128)(2,1)S(1)} fusion(bf16[4,1024,4,128]{1,3,2,0:T(8,128)(2,1)} %copy.57, f32[4,4,128,1024]{3,2,1,0:T(8,128)} %fusion.73, f32[4,4,128,1024]{3,2,1,0:T(8,128)} %get-tuple-element.50, f32[4,4,128]{2,1,0:T(4,128)S(1)} %get-tuple-element.49), kind=kOutput, calls=%fused_computation.40 | convolution fusion | flops 551816192 | bytes 21504000 | tf_op jit(solution)/shard_map/while/body/eval_jaxpr/vmap(hqk,khd->qhd)/dot_general | solution.py:50
  292.8 1.1 copy.72
  293.9 2.5 fusion.49
  296.4 6.0 %collective-permute-done.7 = bf16[4,128,1024]{2,1,0:T(8,128)(2,1)} collective-permute-done((bf16[4,128,1024]{2,1,0:T(8,128)(2,1)}, bf16[4,128,1024]{2,1,0:T(8,128)(2,1)}, u32[]{:S(2)}, u32[]{:S(2)}) %collective-permute-start.7) | collective-permute-done | bytes 1048608 | tf_op jit(solution)/shard_map/ppermute | solution.py:21
  302.5 3.8 fusion.21
  307.2 2.6 fusion.46
  310.9 2.3 fusion.40
  314.6 260.3 %all-reduce.3.cloned.1.call-done = (f32[512,1536]{1,0:T(8,128)}, f32[512,512]{1,0:T(8,128)}) async-done(((f32[512,1536]{1,0:T(8,128)}, f32[512,512]{1,0:T(8,128)}), (f32[512,1536]{1,0:T(8,128)}, f32[512,512]{1,0:T(8,128)})) %all-reduce.3.cloned.1.call-update) | async-done | bytes 4194320 | tf_op jit(solution)/shard_map/psum | solution.py:145
  574.9 4.0 broadcast_multiply_fusion
  (49 shorter events, 11.5 us)
Async XLA Ops:
  7.2 1.6 copy-start
  7.2 14.4 %copy-start.7 = (s32[256,8]{0,1:T(8,128)S(1)}, s32[256,8]{0,1:T(8,128)}, u32[]{:S(2)}) copy-start(s32[256,8]{0,1:T(8,128)} %param.10) | copy-start | bytes 24580
  7.2 14.4 %copy-start.8 = (s32[256,8]{0,1:T(8,128)S(1)}, s32[256,8]{0,1:T(8,128)}, u32[]{:S(2)}) copy-start(s32[256,8]{0,1:T(8,128)} %param.11) | copy-start | bytes 24580
  7.2 567.7 %all-reduce.3.cloned.1.call-start = ((), (), s32[]{:S(2)}) async-start(), calls=%async_computation | async-start | bytes 8388608 | tf_op jit(solution)/shard_map/psum | solution.py:145
  8.8 17.4 %copy-start.2 = (bf16[1,512,512]{2,1,0:T(8,128)(2,1)S(1)}, bf16[1,512,512]{2,1,0:T(8,128)(2,1)}, u32[]{:S(2)}) copy-start(bf16[1,512,512]{2,1,0:T(8,128)(2,1)} %param.7) | copy-start | bytes 1572868
  9.8 1.1 copy-start.5
  12.1 32.1 %collective-permute-start = (bf16[4,128,1024]{2,1,0:T(8,128)(2,1)}, bf16[4,128,1024]{2,1,0:T(8,128)(2,1)}, u32[]{:S(2)}, u32[]{:S(2)}) collective-permute-start(bf16[4,128,1024]{2,1,0:T(8,128)(2,1)} %bitcast.3), channel_id=1, source_target_pairs={{0,8},{4,12},{8,16},{12,20},{16,24},{20,28},{24,32},{28,36},{32,40... | collective-permute-start | bytes 3145736 | tf_op jit(solution)/shard_map/ppermute | solution.py:21
  14.2 34.5 %collective-permute-start.1 = (bf16[4,128,1024]{2,1,0:T(8,128)(2,1)}, bf16[4,128,1024]{2,1,0:T(8,128)(2,1)}, u32[]{:S(2)}, u32[]{:S(2)}) collective-permute-start(bf16[4,128,1024]{2,1,0:T(8,128)(2,1)} %bitcast.3), channel_id=1, source_target_pairs={{0,4},{4,8},{8,12},{12,16},{16,20},{20,24},{24,28},{28,32},{32,36}... | collective-permute-start | bytes 3145736 | tf_op jit(solution)/shard_map/ppermute | solution.py:21
  16.3 34.7 %collective-permute-start.2 = (bf16[4,128,1024]{2,1,0:T(8,128)(2,1)}, bf16[4,128,1024]{2,1,0:T(8,128)(2,1)}, u32[]{:S(2)}, u32[]{:S(2)}) collective-permute-start(bf16[4,128,1024]{2,1,0:T(8,128)(2,1)} %bitcast.3), channel_id=1, source_target_pairs={{0,252},{4,0},{8,4},{12,8},{16,12},{20,16},{24,20},{28,24},{32,28}... | collective-permute-start | bytes 3145736 | tf_op jit(solution)/shard_map/ppermute | solution.py:21
  16.3 37.0 %collective-permute-start.3 = (bf16[4,128,1024]{2,1,0:T(8,128)(2,1)}, bf16[4,128,1024]{2,1,0:T(8,128)(2,1)}, u32[]{:S(2)}, u32[]{:S(2)}) collective-permute-start(bf16[4,128,1024]{2,1,0:T(8,128)(2,1)} %bitcast.3), channel_id=1, source_target_pairs={{0,248},{4,252},{8,0},{12,4},{16,8},{20,12},{24,16},{28,20},{32,24... | collective-permute-start | bytes 3145736 | tf_op jit(solution)/shard_map/ppermute | solution.py:21
  251.0 12.1 %copy-start.1 = (bf16[4,1024,4,128]{1,3,2,0:T(8,128)(2,1)S(1)}, bf16[4,1024,4,128]{1,3,2,0:T(8,128)(2,1)}, u32[]{:S(2)}) copy-start(bf16[4,1024,4,128]{1,3,2,0:T(8,128)(2,1)} %copy.56) | copy-start | bytes 12582916
  253.3 43.1 %collective-permute-start.4 = (bf16[4,128,1024]{2,1,0:T(8,128)(2,1)}, bf16[4,128,1024]{2,1,0:T(8,128)(2,1)}, u32[]{:S(2)}, u32[]{:S(2)}) collective-permute-start(bf16[4,128,1024]{2,1,0:T(8,128)(2,1)} %get-tuple-element.45), channel_id=1, source_target_pairs={{0,248},{4,252},{8,0},{12,4},{16,8},{20,12},{24,16},{28,20},{32,24... | collective-permute-start | bytes 3145736 | tf_op jit(solution)/shard_map/ppermute | solution.py:21
  260.1 36.3 %collective-permute-start.5 = (bf16[4,128,1024]{2,1,0:T(8,128)(2,1)}, bf16[4,128,1024]{2,1,0:T(8,128)(2,1)}, u32[]{:S(2)}, u32[]{:S(2)}) collective-permute-start(bf16[4,128,1024]{2,1,0:T(8,128)(2,1)} %get-tuple-element.48), channel_id=1, source_target_pairs={{0,252},{4,0},{8,4},{12,8},{16,12},{20,16},{24,20},{28,24},{32,28}... | collective-permute-start | bytes 3145736 | tf_op jit(solution)/shard_map/ppermute | solution.py:21
  262.8 33.6 %collective-permute-start.6 = (bf16[4,128,1024]{2,1,0:T(8,128)(2,1)}, bf16[4,128,1024]{2,1,0:T(8,128)(2,1)}, u32[]{:S(2)}, u32[]{:S(2)}) collective-permute-start(bf16[4,128,1024]{2,1,0:T(8,128)(2,1)} %get-tuple-element.47), channel_id=1, source_target_pairs={{0,4},{4,8},{8,12},{12,16},{16,20},{20,24},{24,28},{28,32},{32,36}... | collective-permute-start | bytes 3145736 | tf_op jit(solution)/shard_map/ppermute | solution.py:21
  262.9 39.5 %collective-permute-start.7 = (bf16[4,128,1024]{2,1,0:T(8,128)(2,1)}, bf16[4,128,1024]{2,1,0:T(8,128)(2,1)}, u32[]{:S(2)}, u32[]{:S(2)}) collective-permute-start(bf16[4,128,1024]{2,1,0:T(8,128)(2,1)} %get-tuple-element.46), channel_id=1, source_target_pairs={{0,8},{4,12},{8,16},{12,20},{16,24},{20,28},{24,32},{28,36},{32,40... | collective-permute-start | bytes 3145736 | tf_op jit(solution)/shard_map/ppermute | solution.py:21
  306.3 1.0 copy-start.3
  310.9 2.3 copy-start.4
  574.9 4.0 copy-start.6
Sparse Core Ops, SparseCore 0:
  310.0 264.8 all-reduce.2
where the time goes:
time: 590 us; the launch traced here: 587 us
  waiting for transfers between devices  281 us (48%)
  local copies, waits for them, and re-layouts  118 us (20%)
  matrix products  85 us (14%)
  other arithmetic  69.6 us (12%)
  starting transfers between devices  19.3 us (3%)
  between operations  14.2 us (2%)
    psum x1, waiting for transfers between devices, on_device(): lax.psum((local_qkv, local_out), ('patch', 'sample'))  260 us
    scatter-add x1, other arithmetic, advance(): running.at[flat_slots]  36.2 us
    dot_general x1, matrix products, tile_backward(): jnp.einsum('hqk,qhd->khd', dscore, query_heads, preferred_element_type=jn...  24 us
    dot_general x1, matrix products, tile_backward(): jnp.einsum('hqk,khd->qhd', dscore, key_heads, preferred_element_type=jnp....  22.9 us
    concatenate x2, local copies, waits for them, and re-layouts, tile_backward(): return (attended, dquery, jnp.concatenate([dkey, dvalue], -1))  20.6 us
    ppermute x8, waiting for transfers between devices, from_behind(): return lax.ppermute(value, axis, pairs)  20.2 us
    ppermute x8, starting transfers between devices, from_behind(): return lax.ppermute(value, axis, pairs)  19.3 us
    unnamed x28, local copies, waits for them, and re-layouts  15.8 us
  transfers between devices with their start and end apart: 9, of which 4 were waited for; matrix products, arithmetic and copies ran while one was open for 9% of the time, Pallas kernels for 0%

commit v1 on v0

v1 whole, which is shorter than its diff:
```python
import functools

import jax
import jax.numpy as jnp
from jax import lax
from jax.experimental import pallas as pl
from jax.experimental.pallas import tpu as pltpu
from jax.sharding import PartitionSpec as P

HEADS = 4
TILE = 128
LOCAL = 4
REACH = 2
OFFSETS = [-2, -1, 1, 2]
CHIPS_Y = 4
EPS = 1e-06
MESH = pl.DeviceIdType.MESH
F32 = jnp.float32
BF16 = jnp.bfloat16
LOG2E = 1.4426950408889634

ROWS = LOCAL * TILE
HALO = 2 * TILE
ALL = ROWS + len(OFFSETS) * HALO
D = 512
HW = D // HEADS


def nn(a, b):
    return lax.dot_general(a, b, (((1,), (0,)), ((), ())), preferred_element_type=F32)


def nt(a, b):
    return lax.dot_general(a, b, (((1,), (1,)), ((), ())), preferred_element_type=F32)


def tt(a, b):
    return lax.dot_general(a, b, (((0,), (1,)), ((), ())), preferred_element_type=F32)


def tn(a, b):
    return lax.dot_general(a, b, (((0,), (0,)), ((), ())), preferred_element_type=F32)


def normalise(rows):
    wide = rows.astype(F32)
    inverse = lax.rsqrt(jnp.mean(wide * wide, -1, keepdims=True) + EPS)
    return wide, inverse


def kernel(
    dims,
    kt,
    tv,
    x_ref,
    c_ref,
    w_ref,
    wo_ref,
    gf_ref,
    out_ref,
    stage,
    halo,
    normed_t,
    q,
    k,
    v,
    ga,
    q_t,
    ga_t,
    bias,
    prob,
    dscore,
    attended,
    dquery,
    dkv_t,
    back_out,
    back_in,
    local,
    got0,
    sum0,
    got1,
    sum1,
    got2,
    got3,
    res,
    halo_send,
    halo_recv,
    back_send,
    back_recv,
    red_send,
    red_recv,
    out_sem,
):
    patches, nz, ny, nx = dims
    p = lax.axis_index("patch")
    sx = lax.axis_index("sample")
    core = lax.rem(p, 2)
    y = lax.rem(lax.div(p, 2), ny)
    z = lax.div(p, 2 * ny)

    def patch_at(zz, yy):
        return (zz * ny + yy) * 2 + core

    def first(j):
        return (
            patch_at(z, lax.rem(y + j * core, ny)),
            lax.rem(sx + j * (1 - core), nx),
        )

    def second(j):
        return (
            patch_at(z, lax.rem(y + j * (1 - core), ny)),
            lax.rem(sx + j * core, nx),
        )

    def along_z(j):
        return (patch_at(lax.rem(z + j, nz), y), sx)

    pair = (p + 1 - 2 * core, sx)
    m1 = sx * (1 - core) + y * core
    m2 = sx * core + y * (1 - core)
    group = nx

    barrier = pltpu.get_barrier_semaphore()
    greeted = (
        [(lax.rem(p + o + patches, patches), sx) for o in OFFSETS]
        + [pair]
        + [first(j) for j in range(1, group)]
        + [second(j) for j in range(1, group)]
        + [along_z(j) for j in range(1, nz)]
    )
    for device in greeted:
        pl.semaphore_signal(barrier, inc=1, device_id=device, device_id_type=MESH)

    named = []
    for oi, o in enumerate(OFFSETS):
        row = lax.rem(p - o + patches, patches) * LOCAL
        one = kt[row, LOCAL + oi]
        two = one
        for r in range(1, LOCAL):
            entry = kt[row + r, LOCAL + oi]
            two = jnp.where(entry != one, entry, two)
        named.append((one - p * LOCAL, two - p * LOCAL))
        for s in range(2):
            tile = x_ref[0, 0:TILE, :]
            for r in range(1, LOCAL):
                tile = jnp.where(named[oi][s] == r, x_ref[0, r * TILE : (r + 1) * TILE, :], tile)
            stage[oi, s * TILE : (s + 1) * TILE, :] = tile

    pl.semaphore_wait(barrier, len(greeted))

    def halo_copy(oi):
        return pltpu.make_async_remote_copy(
            src_ref=stage.at[oi],
            dst_ref=halo.at[oi],
            send_sem=halo_send.at[oi],
            recv_sem=halo_recv.at[oi],
            device_id=(lax.rem(p - OFFSETS[oi] + patches, patches), sx),
            device_id_type=MESH,
        )

    def back_copy(oi):
        return pltpu.make_async_remote_copy(
            src_ref=back_out.at[oi],
            dst_ref=back_in.at[oi],
            send_sem=back_send.at[oi],
            recv_sem=back_recv.at[oi],
            device_id=(lax.rem(p + OFFSETS[oi] + patches, patches), sx),
            device_id_type=MESH,
        )

    for oi in (0, 3, 1, 2):
        halo_copy(oi).start()

    base = p * LOCAL
    pick = []
    for t in range(LOCAL):
        pick.append(
            [
                jnp.where(kt[base + t, LOCAL + n] != kt[base, LOCAL + n], 1, 0)
                for n in range(len(OFFSETS))
            ]
        )
        for r in range(LOCAL):
            flag = jnp.int32(0)
            for j in range(LOCAL):
                flag = flag + jnp.where(kt[base + t, j] == base + r, tv[base + t, j], 0)
            low = jnp.where(flag > 0, jnp.float32(0.0), jnp.float32(-1e30))
            bias[t, :, r * TILE : (r + 1) * TILE] = jnp.full((8, TILE), low, F32)
        for n in range(len(OFFSETS)):
            flag = tv[base + t, LOCAL + n]
            low = jnp.where(flag > 0, jnp.float32(0.0), jnp.float32(-1e30))
            bias[t, :, ROWS + n * TILE : ROWS + (n + 1) * TILE] = jnp.full((8, TILE), low, F32)

    wide, inverse = normalise(x_ref[0])
    low = (wide * inverse).astype(BF16)
    normed_t[:, 0:ROWS] = low.T
    for part, target in ((0, q), (1, k), (2, v)):
        for half in range(2):
            at = part * D + half * 2 * HW
            got = nn(low, w_ref[:, at : at + 2 * HW]).astype(BF16)
            for i in range(2):
                piece = got[:, i * HW : (i + 1) * HW]
                target[half * 2 + i, 0:ROWS, :] = piece
                if part == 0:
                    q_t[half * 2 + i] = piece.T
    for half in range(2):
        at = half * 2 * HW
        got = nt(c_ref[0], wo_ref[at : at + 2 * HW, :]).astype(BF16)
        for i in range(2):
            piece = got[:, i * HW : (i + 1) * HW]
            ga[half * 2 + i] = piece
            ga_t[half * 2 + i] = piece.T

    for oi in range(len(OFFSETS)):
        halo_copy(oi).wait_recv()
        wide, inverse = normalise(halo[oi])
        low = (wide * inverse).astype(BF16)
        at_row = ROWS + oi * HALO
        normed_t[:, at_row : at_row + HALO] = low.T
        for part, target in ((1, k), (2, v)):
            for half in range(2):
                at = part * D + half * 2 * HW
                got = nn(low, w_ref[:, at : at + 2 * HW]).astype(BF16)
                for i in range(2):
                    target[half * 2 + i, at_row : at_row + HALO, :] = got[:, i * HW : (i + 1) * HW]

    half_rows = D // 2
    piece1 = half_rows // group
    piece2 = piece1 // group
    base_row = core * half_rows

    def move(h, index, src, dst, device):
        return pltpu.make_async_remote_copy(
            src_ref=src,
            dst_ref=dst,
            send_sem=red_send.at[h, index],
            recv_sem=red_recv.at[h, index],
            device_id=device,
            device_id_type=MESH,
        )

    def rows_at(start, size):
        return pl.ds(pl.multiple_of(start, 16), size)

    at1 = base_row + m1 * piece1
    at2 = at1 + m2 * piece2
    n1 = group - 1
    first_z = 1 + 2 * n1

    def copies(h, phase):
        if phase == 0:
            src = local.at[h, rows_at((1 - core) * half_rows, half_rows), :]
            return [move(h, 0, src, got0.at[h], pair)]
        if phase == 1:
            return [
                move(
                    h,
                    j,
                    sum0.at[h, rows_at(lax.rem(m1 + j, group) * piece1, piece1), :],
                    got1.at[h, j - 1],
                    first(j),
                )
                for j in range(1, group)
            ]
        if phase == 2:
            return [
                move(
                    h,
                    n1 + j,
                    sum1.at[h, rows_at(lax.rem(m2 + j, group) * piece2, piece2), :],
                    got2.at[h, j - 1],
                    second(j),
                )
                for j in range(1, group)
            ]
        if phase == 3:
            mine = got3.at[h, z]
            return [move(h, first_z + j - 1, mine, mine, along_z(j)) for j in range(1, nz)]
        if phase == 4:
            mine = res.at[h, rows_at(at2, piece2), :]
            return [
                move(h, first_z + nz - 2 + j, mine, mine, second(j)) for j in range(1, group)
            ]
        if phase == 5:
            mine = res.at[h, rows_at(at1, piece1), :]
            return [
                move(h, first_z + nz - 2 + n1 + j, mine, mine, first(j))
                for j in range(1, group)
            ]
        mine = res.at[h, rows_at(base_row, half_rows), :]
        return [move(h, first_z + nz - 2 + 2 * n1 + 1, mine, mine, pair)]

    def start(h, phase):
        for copy in copies(h, phase):
            copy.start()

    def advance(h, phase):
        for copy in copies(h, phase):
            copy.wait_recv()
        if phase == 0:
            mine = local[h, rows_at(base_row, half_rows), :].astype(F32)
            sum0[h] = (mine + got0[h].astype(F32)).astype(BF16)
        if phase == 1:
            total = sum0[h, rows_at(m1 * piece1, piece1), :].astype(F32)
            for j in range(group - 1):
                total = total + got1[h, j].astype(F32)
            sum1[h] = total.astype(BF16)
        if phase == 2:
            total = sum1[h, rows_at(m2 * piece2, piece2), :].astype(F32)
            for j in range(group - 1):
                total = total + got2[h, j].astype(F32)
            got3[h, z] = total.astype(BF16)
        if phase == 3:
            total = got3[h, 0].astype(F32)
            for j in range(1, nz):
                total = total + got3[h, j].astype(F32)
            res[h, rows_at(at2, piece2), :] = total.astype(BF16)
        if phase < 6:
            start(h, phase + 1)

    scaling = HW ** (-0.5)

    def head(h, carry):
        for t in range(LOCAL):
            rows = slice(t * TILE, (t + 1) * TILE)

            def chosen(ref):
                parts = [ref[h, 0:ROWS, :]]
                for n in range(len(OFFSETS)):
                    at = ROWS + n * HALO
                    near = ref[h, at : at + TILE, :]
                    far = ref[h, at + TILE : at + HALO, :]
                    parts.append(jnp.where(pick[t][n] == 0, near, far))
                return jnp.concatenate(parts, 0)

            keys = chosen(k)
            values = chosen(v)
            scores = nt(q[h, rows, :], keys) + bias[t, 0:1, :]
            highest = jnp.max(scores, -1, keepdims=True)
            expanded = jnp.exp2((scores - highest) * (scaling * LOG2E))
            attention = expanded * (1.0 / jnp.sum(expanded, -1, keepdims=True))
            attention_low = attention.astype(BF16)
            dprob = nt(ga[h, rows, :], values)
            centre = jnp.sum(attention * dprob, -1, keepdims=True)
            ds = (attention * (dprob - centre) * scaling).astype(BF16)
            attended[h, rows, :] = nn(attention_low, values).astype(BF16)
            dquery[h, rows, :] = nn(ds, keys).astype(BF16)
            for full, piece in ((prob, attention_low), (dscore, ds)):
                full[rows, 0:ROWS] = piece[:, 0:ROWS]
                for n in range(len(OFFSETS)):
                    part = piece[:, ROWS + n * TILE : ROWS + (n + 1) * TILE]
                    for s in range(2):
                        at = ROWS + (2 * n + s) * TILE
                        keep = jnp.where(pick[t][n] == s, 1.0, 0.0).astype(BF16)
                        full[rows, at : at + TILE] = part * keep

            @pl.when(h >= 1)
            def _():
                advance(h - 1, t)

            if t < 2:

                @pl.when(h >= 2)
                def _():
                    advance(h - 2, 4 + t)

        at = pl.multiple_of(h * HW, HW)
        dk = nn(q_t[h], dscore[...]).astype(BF16)
        dv = nn(ga_t[h], prob[...]).astype(BF16)
        dkv_t[pl.ds(at, HW), :] = dk
        dkv_t[pl.ds(pl.multiple_of(D + h * HW, HW), HW), :] = dv
        local[h, :, 0:HW] = nn(normed_t[:, 0:ROWS], dquery[h]).astype(BF16)
        local[h, :, HW : 2 * HW] = nt(normed_t[...], dk).astype(BF16)
        local[h, :, 2 * HW : 3 * HW] = nt(normed_t[...], dv).astype(BF16)
        outer = tn(attended[h], c_ref[0]).astype(BF16)
        for r in range(D // HW):
            local[h, r * HW : (r + 1) * HW, 3 * HW :] = outer[:, r * HW : (r + 1) * HW]
        start(h, 0)
        return carry

    lax.fori_loop(0, HEADS, head, 0)

    def give_back(oi):
        at = ROWS + oi * HALO
        back_out[oi] = tt(dkv_t[:, at : at + HALO], w_ref[:, D:]).astype(BF16)
        back_copy(oi).start()

    last = HEADS - 1
    advance(last - 1, 4)
    give_back(0)
    give_back(3)
    advance(last, 0)
    give_back(1)
    give_back(2)
    advance(last, 1)
    advance(last - 1, 5)
    grad = tt(dkv_t[:, 0:ROWS], w_ref[:, D:])
    for h in range(HEADS):
        grad = grad + nt(dquery[h], w_ref[:, h * HW : (h + 1) * HW])
    advance(last, 2)

    def out_copy(h):
        return pltpu.make_async_copy(res.at[h], out_ref.at[h], out_sem.at[h])

    for h in range(HEADS - 1):
        advance(h, 6)
        out_copy(h).start()
    advance(last, 3)
    for oi in range(len(OFFSETS)):
        back_copy(oi).wait_recv()
    advance(last, 4)
    for r in range(LOCAL):
        rows = slice(r * TILE, (r + 1) * TILE)
        total = grad[rows]
        for oi in range(len(OFFSETS)):
            for s in range(2):
                came = back_in[oi, s * TILE : (s + 1) * TILE, :].astype(F32)
                total = total + jnp.where(named[oi][s] == r, came, 0.0)
        wide, inverse = normalise(x_ref[0, rows, :])
        normed = wide * inverse
        mean = jnp.mean(total * normed, -1, keepdims=True)
        result = c_ref[0, rows, :].astype(F32) + inverse * (total - normed * mean)
        gf_ref[0, rows, :] = result.astype(BF16)
    advance(last, 5)
    advance(last, 6)
    out_copy(last).start()
    for oi in range(len(OFFSETS)):
        halo_copy(oi).wait_send()
        back_copy(oi).wait_send()

    def settle(h, carry):
        for phase in range(7):
            for copy in copies(h, phase):
                copy.wait_send()
        return carry

    lax.fori_loop(0, HEADS, settle, 0)
    for h in range(HEADS):
        out_copy(h).wait()


def on_device(dims, features, cotangent, weight_qkv, weight_out, key_tiles, tile_valid):
    patches, nz, ny, nx = dims
    group = nx
    half_rows = D // 2
    piece1 = half_rows // group
    piece2 = piece1 // group
    n_sem = 1 + 4 * (group - 1) + nz - 1 + 1
    n_off = len(OFFSETS)
    vmem = pl.BlockSpec(memory_space=pltpu.VMEM)
    smem = pl.BlockSpec(memory_space=pltpu.SMEM)
    grad_features, gathered = pl.pallas_call(
        functools.partial(kernel, dims),
        out_shape=(
            jax.ShapeDtypeStruct((1, ROWS, D), BF16),
            jax.ShapeDtypeStruct((HEADS, D, D), BF16),
        ),
        in_specs=[smem, smem, vmem, vmem, vmem, vmem],
        out_specs=(vmem, pl.BlockSpec(memory_space=pl.ANY)),
        scratch_shapes=[
            pltpu.VMEM((n_off, HALO, D), BF16),
            pltpu.VMEM((n_off, HALO, D), BF16),
            pltpu.VMEM((D, ALL), BF16),
            pltpu.VMEM((HEADS, ROWS, HW), BF16),
            pltpu.VMEM((HEADS, ALL, HW), BF16),
            pltpu.VMEM((HEADS, ALL, HW), BF16),
            pltpu.VMEM((HEADS, ROWS, HW), BF16),
            pltpu.VMEM((HEADS, HW, ROWS), BF16),
            pltpu.VMEM((HEADS, HW, ROWS), BF16),
            pltpu.VMEM((LOCAL, 8, 2 * ROWS), F32),
            pltpu.VMEM((ROWS, ALL), BF16),
            pltpu.VMEM((ROWS, ALL), BF16),
            pltpu.VMEM((HEADS, ROWS, HW), BF16),
            pltpu.VMEM((HEADS, ROWS, HW), BF16),
            pltpu.VMEM((2 * D, ALL), BF16),
            pltpu.VMEM((n_off, HALO, D), BF16),
            pltpu.VMEM((n_off, HALO, D), BF16),
            pltpu.VMEM((HEADS, D, D), BF16),
            pltpu.VMEM((HEADS, half_rows, D), BF16),
            pltpu.VMEM((HEADS, half_rows, D), BF16),
            pltpu.VMEM((HEADS, group - 1, piece1, D), BF16),
            pltpu.VMEM((HEADS, piece1, D), BF16),
            pltpu.VMEM((HEADS, group - 1, piece2, D), BF16),
            pltpu.VMEM((HEADS, nz, piece2, D), BF16),
            pltpu.VMEM((HEADS, D, D), BF16),
            pltpu.SemaphoreType.DMA((n_off,)),
            pltpu.SemaphoreType.DMA((n_off,)),
            pltpu.SemaphoreType.DMA((n_off,)),
            pltpu.SemaphoreType.DMA((n_off,)),
            pltpu.SemaphoreType.DMA((HEADS, n_sem)),
            pltpu.SemaphoreType.DMA((HEADS, n_sem)),
            pltpu.SemaphoreType.DMA((HEADS,)),
        ],
        compiler_params=pltpu.CompilerParams(
            collective_id=0, has_side_effects=True, vmem_limit_bytes=48 * 1024 * 1024
        ),
        cost_estimate=pl.CostEstimate(
            flops=8 * 10**9, bytes_accessed=8 * 2**20, transcendentals=2 * 2**20
        ),
        name="layer",
    )(key_tiles, tile_valid, features, cotangent, weight_qkv, weight_out)
    factor = float(patches * nx * ROWS) ** (-0.5)
    grad_qkv = gathered[:, :, : 3 * HW].reshape(HEADS, D, 3, HW).transpose(1, 2, 0, 3)
    grad_out = gathered[:, :, 3 * HW :].reshape(HEADS, D // HW, HW, HW).transpose(0, 2, 1, 3)
    return (
        grad_features,
        grad_qkv.reshape(D, 3 * D).astype(F32) * factor,
        grad_out.reshape(D, D).astype(F32) * factor,
    )


def solution(mesh):
    patches = mesh.shape["patch"]
    dims = (patches, patches // (2 * CHIPS_Y), CHIPS_Y, mesh.shape["sample"])
    placed = (P("sample", "patch", None), P("sample", "patch", None), P(), P(), P(), P())
    return jax.shard_map(
        functools.partial(on_device, dims),
        mesh=mesh,
        in_specs=placed,
        out_specs=(P("sample", "patch", None), P(), P()),
        check_vma=False,
    )
```

time: 590 us -> 140 us (0.24)
  waiting for transfers between devices: 281 us -> 0 us
  Pallas kernels: 0 us -> 116 us
  local copies, waits for them, and re-layouts: 118 us -> 19.6 us
  matrix products: 85 us -> 0 us
  other arithmetic: 69.6 us -> 2.04 us
  starting transfers between devices: 19.3 us -> 0 us
  between operations: 14.2 us -> 0.68 us
    psum x1 -> x0, waiting for transfers between devices: 260 us -> none  [on_device(): lax.psum((local_qkv, local_out), ('patch', 'sample'))]
    pallas_call x0 -> x1, Pallas kernels: none -> 116 us  [on_device(): pl.pallas_call(functools.partial(kernel, dims), out_shape=(jax.ShapeDtype...]
    dot_general x10 -> x0, matrix products: 76.2 us -> none  [the longest x1 24 us: tile_backward(): jnp.einsum('hqk,qhd->khd', dscore, query_heads, preferred_element_type=jn...]
    scatter-add x1 -> x0, other arithmetic: 36.2 us -> none  [advance(): running.at[flat_slots]]
    reshape x9 -> x0, local copies, waits for them, and re-layouts: 34.1 us -> none  [the longest x2 14.5 us: tile_backward(): pair_tiles[:, :, :model_width].reshape(-1, head_count, head_width)]
    concatenate x3 -> x0, local copies, waits for them, and re-layouts: 22.8 us -> none  [the longest x2 20.6 us: tile_backward(): return (attended, dquery, jnp.concatenate([dkey, dvalue], -1))]
    transpose x3 -> x0, local copies, waits for them, and re-layouts: 20.8 us -> none  [the longest x1 9.87 us: tile_backward(): jnp.einsum('hqk,qhd->khd', dscore, query_heads, preferred_element_type=jn...]
    ppermute x8 -> x0, waiting for transfers between devices: 20.2 us -> none  [from_behind(): return lax.ppermute(value, axis, pairs)]
  transfers between devices with their start and end apart: 9 -> 0, of which waited for: 4 -> 0; matrix products, arithmetic and copies ran while one was open for 9% -> 0% of each run, Pallas kernels for 0% -> 0%
where the time goes in v1:
time: 140 us; the launch traced here: 139 us
  Pallas kernels  116 us (83%)
  local copies, waits for them, and re-layouts  19.6 us (14%)
  other arithmetic  2.04 us (1%)
    pallas_call x1, Pallas kernels, on_device(): pl.pallas_call(functools.partial(kernel, dims), out_shape=(jax.ShapeDtype...  116 us
    unnamed x13, local copies, waits for them, and re-layouts  11.5 us
    mul x2, local copies, waits for them, and re-layouts, on_device(): grad_qkv.reshape(D, 3 * D).astype(F32) * factor  7.39 us

profile of v1, /device:TPU:1, one launch (start us, length us, event | category | flops | bytes accessed | tf_op | source)
XLA Modules:
  0.0 138.7 jit_solution(9170336920917684981)
XLA Ops:
  0.6 0.8 copy.17.kt
  1.5 0.8 copy.18.tv
  2.3 0.0 copy-start
  2.3 1.4 %copy-done = bf16[512,1536]{1,0:T(8,128)(2,1)S(1)} copy-done((bf16[512,1536]{1,0:T(8,128)(2,1)S(1)}, bf16[512,1536]{1,0:T(8,128)(2,1)}, u32[]{:S(2)}) %copy-start) | copy-done | bytes 1572888
  3.7 0.0 copy-start.1
  3.7 1.0 copy-done.1
  4.7 0.0 copy-start.2
  4.7 1.0 copy-done.2
  5.8 0.0 copy-start.3
  5.8 1.0 copy-done.3
  6.8 116.4 %layer.1 = (bf16[1,512,512]{2,1,0:T(8,128)(2,1)S(1)}, bf16[4,512,512]{2,1,0:T(8,128)(2,1)S(1)}) custom-call(s32[256,8]{1,0:T(8,128)S(1)} %copy.17.kt, s32[256,8]{1,0:T(8,128)S(1)} %copy.18.tv, bf16[1,512,512]{2,1,0:T(8,128)(2,1)S(1)} %copy-done.1, bf16[1,512,512]{2,1,0:T(8,128)(2,1)S(1)} %copy-done.2, bf16[512,1536]{1,0:T(8,128)(2,1)S(1)} %copy-done, ...), custom_call_target="tpu_custom_call" | custom-call | flops 8000000000 | bytes 8388608 | tf_op jit(solution)/shard_map/layer/pallas_call | solution.py:453
  123.2 0.1 convert_multiply_fusion.1
  123.3 0.7 copy.21
  124.0 1.0 copy.25
  125.0 1.9 %convert_multiply_fusion = f32[4,512,384]{2,1,0:T(8,128)} fusion(bf16[4,512,512]{2,1,0:T(8,128)(2,1)S(1)} %get-tuple-element.6), kind=kLoop, calls=%fused_computation | loop fusion | flops 1572864 | bytes 4718592 | tf_op jit(solution)/shard_map/mul | solution.py:508
  127.0 3.5 %copy.19 = f32[4,512,384]{1,2,0:T(8,128)} copy(f32[4,512,384]{2,1,0:T(8,128)} %convert_multiply_fusion) | data formatting | bytes 6291456 | tf_op jit(solution)/shard_map/mul | solution.py:508
  130.5 3.9 %copy.20 = f32[512,3,4,128]{0,3,2,1:T(8,128)} copy(f32[512,3,4,128]{0,3,1,2:T(8,128)} %bitcast.12) | data formatting | bytes 6291456 | tf_op jit(solution)/shard_map/mul | solution.py:508
  134.3 3.5 %copy.22 = f32[512,1536]{1,0:T(8,128)} copy(f32[512,1536]{0,1:T(8,128)} %bitcast.13) | data formatting | bytes 6291456
  137.9 0.8 copy.27
Async XLA Ops:
  2.3 1.4 %copy-start = (bf16[512,1536]{1,0:T(8,128)(2,1)S(1)}, bf16[512,1536]{1,0:T(8,128)(2,1)}, u32[]{:S(2)}) copy-start(bf16[512,1536]{1,0:T(8,128)(2,1)} %w_ref.1) | copy-start | bytes 4718596
  3.7 1.0 copy-start.1
  4.7 1.0 copy-start.2
  5.8 1.0 copy-start.3

commit v2 on v1

--- a/solution.py
+++ b/solution.py
@@ -18,12 +18,18 @@
 F32 = jnp.float32
 BF16 = jnp.bfloat16
 LOG2E = 1.4426950408889634
+BETWEEN = []
+AFTER = [0, 3, (0, 0), 1, 2, (0, 1), "own", (0, 2), (0, 3), "finish", (0, 4), (0, 5), (0, 6), (0, 7)]
+
 
 ROWS = LOCAL * TILE
 HALO = 2 * TILE
 ALL = ROWS + len(OFFSETS) * HALO
 D = 512
 HW = D // HEADS
+PER_CHUNK = 4
+CHUNKS = HEADS // PER_CHUNK
+CHUNK_ROWS = PER_CHUNK * D
 
 
 def nn(a, b):
@@ -52,12 +58,17 @@
     dims,
     kt,
     tv,
+    x_hbm,
+    c_hbm,
+    w_hbm,
+    wo_hbm,
+    gf_hbm,
+    out_ref,
+    gf_ref,
     x_ref,
     c_ref,
     w_ref,
     wo_ref,
-    gf_ref,
-    out_ref,
     stage,
     halo,
     normed_t,
@@ -81,6 +92,7 @@
     got1,
     sum1,
     got2,
+    sum2,
     got3,
     res,
     halo_send,
@@ -90,6 +102,7 @@
     red_send,
     red_recv,
     out_sem,
+    in_sem,
 ):
     patches, nz, ny, nx = dims
     p = lax.axis_index("patch")
@@ -120,6 +133,15 @@
     m1 = sx * (1 - core) + y * core
     m2 = sx * core + y * (1 - core)
     group = nx
+
+    loads = [
+        pltpu.make_async_copy(src, dst, in_sem.at[i])
+        for i, (src, dst) in enumerate(
+            ((x_hbm, x_ref), (w_hbm, w_ref), (c_hbm, c_ref), (wo_hbm, wo_ref))
+        )
+    ]
+    for load in loads:
+        load.start()
 
     barrier = pltpu.get_barrier_semaphore()
     greeted = (
@@ -132,6 +154,7 @@
     for device in greeted:
         pl.semaphore_signal(barrier, inc=1, device_id=device, device_id_type=MESH)
 
+    loads[0].wait()
     named = []
     for oi, o in enumerate(OFFSETS):
         row = lax.rem(p - o + patches, patches) * LOCAL
@@ -192,6 +215,7 @@
             low = jnp.where(flag > 0, jnp.float32(0.0), jnp.float32(-1e30))
             bias[t, :, ROWS + n * TILE : ROWS + (n + 1) * TILE] = jnp.full((8, TILE), low, F32)
 
+    loads[1].wait()
     wide, inverse = normalise(x_ref[0])
     low = (wide * inverse).astype(BF16)
     normed_t[:, 0:ROWS] = low.T
@@ -204,6 +228,8 @@
                 target[half * 2 + i, 0:ROWS, :] = piece
                 if part == 0:
                     q_t[half * 2 + i] = piece.T
+    loads[2].wait()
+    loads[3].wait()
     for half in range(2):
         at = half * 2 * HW
         got = nt(c_ref[0], wo_ref[at : at + 2 * HW, :]).astype(BF16)
@@ -225,99 +251,108 @@
                 for i in range(2):
                     target[half * 2 + i, at_row : at_row + HALO, :] = got[:, i * HW : (i + 1) * HW]
 
-    half_rows = D // 2
+    half_rows = CHUNK_ROWS // 2
     piece1 = half_rows // group
     piece2 = piece1 // group
+    down, across = split_last(piece2, nz)
+    piece3, width3 = piece2 // down, D // across
     base_row = core * half_rows
-
-    def move(h, index, src, dst, device):
-        return pltpu.make_async_remote_copy(
-            src_ref=src,
-            dst_ref=dst,
-            send_sem=red_send.at[h, index],
-            recv_sem=red_recv.at[h, index],
-            device_id=device,
-            device_id_type=MESH,
-        )
-
-    def rows_at(start, size):
-        return pl.ds(pl.multiple_of(start, 16), size)
-
     at1 = base_row + m1 * piece1
     at2 = at1 + m2 * piece2
     n1 = group - 1
-    first_z = 1 + 2 * n1
-
-    def copies(h, phase):
+    counts = [1, n1, n1, nz - 1, nz - 1, n1, n1, 1]
+    offsets = [sum(counts[:i]) for i in range(len(counts))]
+
+    def rows_at(start, size):
+        return pl.ds(pl.multiple_of(start, 16), size)
+
+    def last_piece(index, start):
+        return (
+            rows_at(start + lax.div(index, across) * piece3, piece3),
+            pl.ds(pl.multiple_of(lax.rem(index, across) * width3, 128), width3),
+        )
+
+    def copies(g, phase):
         if phase == 0:
-            src = local.at[h, rows_at((1 - core) * half_rows, half_rows), :]
-            return [move(h, 0, src, got0.at[h], pair)]
-        if phase == 1:
-            return [
-                move(
-                    h,
-                    j,
-                    sum0.at[h, rows_at(lax.rem(m1 + j, group) * piece1, piece1), :],
-                    got1.at[h, j - 1],
+            src = local.at[g, rows_at((1 - core) * half_rows, half_rows), :]
+            moves = [(src, got0.at[g], pair)]
+        elif phase == 1:
+            moves = [
+                (
+                    sum0.at[g, rows_at(lax.rem(m1 + j, group) * piece1, piece1), :],
+                    got1.at[g, j - 1],
                     first(j),
                 )
                 for j in range(1, group)
             ]
-        if phase == 2:
-            return [
-                move(
-                    h,
-                    n1 + j,
-                    sum1.at[h, rows_at(lax.rem(m2 + j, group) * piece2, piece2), :],
-                    got2.at[h, j - 1],
+        elif phase == 2:
+            moves = [
+                (
+                    sum1.at[g, rows_at(lax.rem(m2 + j, group) * piece2, piece2), :],
+                    got2.at[g, j - 1],
                     second(j),
                 )
                 for j in range(1, group)
             ]
-        if phase == 3:
-            mine = got3.at[h, z]
-            return [move(h, first_z + j - 1, mine, mine, along_z(j)) for j in range(1, nz)]
-        if phase == 4:
-            mine = res.at[h, rows_at(at2, piece2), :]
-            return [
-                move(h, first_z + nz - 2 + j, mine, mine, second(j)) for j in range(1, group)
-            ]
-        if phase == 5:
-            mine = res.at[h, rows_at(at1, piece1), :]
-            return [
-                move(h, first_z + nz - 2 + n1 + j, mine, mine, first(j))
-                for j in range(1, group)
-            ]
-        mine = res.at[h, rows_at(base_row, half_rows), :]
-        return [move(h, first_z + nz - 2 + 2 * n1 + 1, mine, mine, pair)]
-
-    def start(h, phase):
-        for copy in copies(h, phase):
+        elif phase == 3:
+            moves = []
+            for j in range(1, nz):
+                at, columns = last_piece(lax.rem(z + j, nz), 0)
+                moves.append((sum2.at[g, at, columns], got3.at[g, j - 1], along_z(j)))
+        elif phase == 4:
+            at, columns = last_piece(z, at2)
+            mine = res.at[g, at, columns]
+            moves = [(mine, mine, along_z(j)) for j in range(1, nz)]
+        elif phase == 5:
+            mine = res.at[g, rows_at(at2, piece2), :]
+            moves = [(mine, mine, second(j)) for j in range(1, group)]
+        elif phase == 6:
+            mine = res.at[g, rows_at(at1, piece1), :]
+            moves = [(mine, mine, first(j)) for j in range(1, group)]
+        else:
+            mine = res.at[g, rows_at(base_row, half_rows), :]
+            moves = [(mine, mine, pair)]
+        return [
+            pltpu.make_async_remote_copy(
+                src_ref=src,
+                dst_ref=dst,
+                send_sem=red_send.at[g, offsets[phase] + i],
+                recv_sem=red_recv.at[g, offsets[phase] + i],
+                device_id=device,
+                device_id_type=MESH,
+            )
+            for i, (src, dst, device) in enumerate(moves)
+        ]
+
+    def start(g, phase):
+        for copy in copies(g, phase):
             copy.start()
 
-    def advance(h, phase):
-        for copy in copies(h, phase):
+    def advance(g, phase):
+        for copy in copies(g, phase):
             copy.wait_recv()
         if phase == 0:
-            mine = local[h, rows_at(base_row, half_rows), :].astype(F32)
-            sum0[h] = (mine + got0[h].astype(F32)).astype(BF16)
+            mine = local[g, rows_at(base_row, half_rows), :].astype(F32)
+            sum0[g] = (mine + got0[g].astype(F32)).astype(BF16)
         if phase == 1:
-            total = sum0[h, rows_at(m1 * piece1, piece1), :].astype(F32)
-            for j in range(group - 1):
-                total = total + got1[h, j].astype(F32)
-            sum1[h] = total.astype(BF16)
+            total = sum0[g, rows_at(m1 * piece1, piece1), :].astype(F32)
+            for j in range(n1):
+                total = total + got1[g, j].astype(F32)
+            sum1[g] = total.astype(BF16)
         if phase == 2:
-            total = sum1[h, rows_at(m2 * piece2, piece2), :].astype(F32)
-            for j in range(group - 1):
-                total = total + got2[h, j].astype(F32)
-            got3[h, z] = total.astype(BF16)
+            total = sum1[g, rows_at(m2 * piece2, piece2), :].astype(F32)
+            for j in range(n1):
+                total = total + got2[g, j].astype(F32)
+            sum2[g] = total.astype(BF16)
         if phase == 3:
-            total = got3[h, 0].astype(F32)
-            for j in range(1, nz):
-                total = total + got3[h, j].astype(F32)
-            res[h, rows_at(at2, piece2), :] = total.astype(BF16)
-        if phase < 6:
-            start(h, phase + 1)
+            at, columns = last_piece(z, 0)
+            total = sum2[g, at, columns].astype(F32)
+            for j in range(nz - 1):
+                total = total + got3[g, j].astype(F32)
+            at, columns = last_piece(z, at2)
+            res[g, at, columns] = total.astype(BF16)
+        if phase < 7:
+            start(g, phase + 1)
 
     scaling = HW ** (-0.5)
 
@@ -355,28 +390,33 @@
                         keep = jnp.where(pick[t][n] == s, 1.0, 0.0).astype(BF16)
                         full[rows, at : at + TILE] = part * keep
 
-            @pl.when(h >= 1)
-            def _():
-                advance(h - 1, t)
-
-            if t < 2:
-
-                @pl.when(h >= 2)
-                def _():
-                    advance(h - 2, 4 + t)
+            for when, g, phase in BETWEEN:
+                if when % LOCAL == t:
+
+                    @pl.when(h == when // LOCAL)
+                    def _():
+                        advance(g, phase)
 
         at = pl.multiple_of(h * HW, HW)
         dk = nn(q_t[h], dscore[...]).astype(BF16)
         dv = nn(ga_t[h], prob[...]).astype(BF16)
         dkv_t[pl.ds(at, HW), :] = dk
         dkv_t[pl.ds(pl.multiple_of(D + h * HW, HW), HW), :] = dv
-        local[h, :, 0:HW] = nn(normed_t[:, 0:ROWS], dquery[h]).astype(BF16)
-        local[h, :, HW : 2 * HW] = nt(normed_t[...], dk).astype(BF16)
-        local[h, :, 2 * HW : 3 * HW] = nt(normed_t[...], dv).astype(BF16)
+        g = lax.div(h, PER_CHUNK)
+        top = lax.rem(h, PER_CHUNK) * D
+        rows = rows_at(top, D)
+        local[g, rows, 0:HW] = nn(normed_t[:, 0:ROWS], dquery[h]).astype(BF16)
+        local[g, rows, HW : 2 * HW] = nt(normed_t[...], dk).astype(BF16)
+        local[g, rows, 2 * HW : 3 * HW] = nt(normed_t[...], dv).astype(BF16)
         outer = tn(attended[h], c_ref[0]).astype(BF16)
         for r in range(D // HW):
-            local[h, r * HW : (r + 1) * HW, 3 * HW :] = outer[:, r * HW : (r + 1) * HW]
-        start(h, 0)
+            rows = rows_at(top + r * HW, HW)
+            local[g, rows, 3 * HW :] = outer[:, r * HW : (r + 1) * HW]
+
+        @pl.when(lax.rem(h, PER_CHUNK) == PER_CHUNK - 1)
+        def _():
+            start(g, 0)
+
         return carry
 
     lax.fori_loop(0, HEADS, head, 0)
@@ -386,79 +426,103 @@
         back_out[oi] = tt(dkv_t[:, at : at + HALO], w_ref[:, D:]).astype(BF16)
         back_copy(oi).start()
 
-    last = HEADS - 1
-    advance(last - 1, 4)
-    give_back(0)
-    give_back(3)
-    advance(last, 0)
-    give_back(1)
-    give_back(2)
-    advance(last, 1)
-    advance(last - 1, 5)
-    grad = tt(dkv_t[:, 0:ROWS], w_ref[:, D:])
-    for h in range(HEADS):
-        grad = grad + nt(dquery[h], w_ref[:, h * HW : (h + 1) * HW])
-    advance(last, 2)
-
-    def out_copy(h):
-        return pltpu.make_async_copy(res.at[h], out_ref.at[h], out_sem.at[h])
-
-    for h in range(HEADS - 1):
-        advance(h, 6)
-        out_copy(h).start()
-    advance(last, 3)
-    for oi in range(len(OFFSETS)):
-        back_copy(oi).wait_recv()
-    advance(last, 4)
-    for r in range(LOCAL):
-        rows = slice(r * TILE, (r + 1) * TILE)
-        total = grad[rows]
+    last = CHUNKS - 1
+    grad = []
+
+    def own_grad():
+        total = tt(dkv_t[:, 0:ROWS], w_ref[:, D:])
+        for h in range(HEADS):
+            total = total + nt(dquery[h], w_ref[:, h * HW : (h + 1) * HW])
+        grad.append(total)
+
+    def finish_features():
         for oi in range(len(OFFSETS)):
-            for s in range(2):
-                came = back_in[oi, s * TILE : (s + 1) * TILE, :].astype(F32)
-                total = total + jnp.where(named[oi][s] == r, came, 0.0)
-        wide, inverse = normalise(x_ref[0, rows, :])
-        normed = wide * inverse
-        mean = jnp.mean(total * normed, -1, keepdims=True)
-        result = c_ref[0, rows, :].astype(F32) + inverse * (total - normed * mean)
-        gf_ref[0, rows, :] = result.astype(BF16)
-    advance(last, 5)
-    advance(last, 6)
-    out_copy(last).start()
+            back_copy(oi).wait_recv()
+        for r in range(LOCAL):
+            rows = slice(r * TILE, (r + 1) * TILE)
+            total = grad[0][rows]
+            for oi in range(len(OFFSETS)):
+                for s in range(2):
+                    came = back_in[oi, s * TILE : (s + 1) * TILE, :].astype(F32)
+                    total = total + jnp.where(named[oi][s] == r, came, 0.0)
+            wide, inverse = normalise(x_ref[0, rows, :])
+            normed = wide * inverse
+            mean = jnp.mean(total * normed, -1, keepdims=True)
+            result = c_ref[0, rows, :].astype(F32) + inverse * (total - normed * mean)
+            gf_ref[0, rows, :] = result.astype(BF16)
+        features_copy.start()
+
+    def out_copy(g):
+        return pltpu.make_async_copy(res.at[g], out_ref.at[g], out_sem.at[g])
+
+    features_copy = pltpu.make_async_copy(gf_ref, gf_hbm, in_sem.at[4])
+    for step in AFTER:
+        if step == "own":
+            own_grad()
+        elif step == "finish":
+            finish_features()
+        elif isinstance(step, int):
+            give_back(step)
+        else:
+            g, phase = step
+            advance(g, phase)
+            if phase == 7:
+                out_copy(g).start()
     for oi in range(len(OFFSETS)):
         halo_copy(oi).wait_send()
         back_copy(oi).wait_send()
 
-    def settle(h, carry):
-        for phase in range(7):
-            for copy in copies(h, phase):
+    def settle(g, carry):
+        for phase in range(8):
+            for copy in copies(g, phase):
                 copy.wait_send()
         return carry
 
-    lax.fori_loop(0, HEADS, settle, 0)
+    lax.fori_loop(0, CHUNKS, settle, 0)
+    for g in range(CHUNKS):
+        out_copy(g).wait()
+    features_copy.wait()
+
+
+def split_last(rows, count):
+    down = min(count, rows // 16)
+    return down, count // down
+
+
+def finish(factor, chunks, features, qkv, out, grad_features):
     for h in range(HEADS):
-        out_copy(h).wait()
+        for part in range(3):
+            piece = chunks[h, :, part * HW : (part + 1) * HW]
+            at = part * D + h * HW
+            qkv[:, at : at + HW] = piece.astype(F32) * factor
+        out[h * HW : (h + 1) * HW, :] = chunks[h, :, 3 * HW :].astype(F32) * factor
+    grad_features[...] = features[...]
 
 
 def on_device(dims, features, cotangent, weight_qkv, weight_out, key_tiles, tile_valid):
     patches, nz, ny, nx = dims
     group = nx
-    half_rows = D // 2
+    half_rows = CHUNK_ROWS // 2
     piece1 = half_rows // group
     piece2 = piece1 // group
-    n_sem = 1 + 4 * (group - 1) + nz - 1 + 1
+    down, across = split_last(piece2, nz)
+    n_sem = 2 + 4 * (group - 1) + 2 * (nz - 1)
     n_off = len(OFFSETS)
-    vmem = pl.BlockSpec(memory_space=pltpu.VMEM)
     smem = pl.BlockSpec(memory_space=pltpu.SMEM)
     grad_features, gathered = pl.pallas_call(
         functools.partial(kernel, dims),
         out_shape=(
             jax.ShapeDtypeStruct((1, ROWS, D), BF16),
-            jax.ShapeDtypeStruct((HEADS, D, D), BF16),
+            jax.ShapeDtypeStruct((CHUNKS, CHUNK_ROWS, D), BF16),
         ),
-        in_specs=[smem, smem, vmem, vmem, vmem, vmem],
-        out_specs=(vmem, pl.BlockSpec(memory_space=pl.ANY)),
+        in_specs=[smem, smem] + [pl.BlockSpec(memory_space=pltpu.HBM)] * 4,
+        out_specs=(pl.BlockSpec(memory_space=pl.ANY), pl.BlockSpec(memory_space=pl.ANY)),
         scratch_shapes=[
+            pltpu.VMEM((1, ROWS, D), BF16),
+            pltpu.VMEM((1, ROWS, D), BF16),
+            pltpu.VMEM((1, ROWS, D), BF16),
+            pltpu.VMEM((D, 3 * D), BF16),
+            pltpu.VMEM((D, D), BF16),
             pltpu.VMEM((n_off, HALO, D), BF16),
             pltpu.VMEM((n_off, HALO, D), BF16),
             pltpu.VMEM((D, ALL), BF16),
@@ -476,24 +540,26 @@
             pltpu.VMEM((2 * D, ALL), BF16),
             pltpu.VMEM((n_off, HALO, D), BF16),
             pltpu.VMEM((n_off, HALO, D), BF16),
-            pltpu.VMEM((HEADS, D, D), BF16),
-            pltpu.VMEM((HEADS, half_rows, D), BF16),
-            pltpu.VMEM((HEADS, half_rows, D), BF16),
-            pltpu.VMEM((HEADS, group - 1, piece1, D), BF16),
-            pltpu.VMEM((HEADS, piece1, D), BF16),
-            pltpu.VMEM((HEADS, group - 1, piece2, D), BF16),
-            pltpu.VMEM((HEADS, nz, piece2, D), BF16),
-            pltpu.VMEM((HEADS, D, D), BF16),
+            pltpu.VMEM((CHUNKS, CHUNK_ROWS, D), BF16),
+            pltpu.VMEM((CHUNKS, half_rows, D), BF16),
+            pltpu.VMEM((CHUNKS, half_rows, D), BF16),
+            pltpu.VMEM((CHUNKS, group - 1, piece1, D), BF16),
+            pltpu.VMEM((CHUNKS, piece1, D), BF16),
+            pltpu.VMEM((CHUNKS, group - 1, piece2, D), BF16),
+            pltpu.VMEM((CHUNKS, piece2, D), BF16),
+            pltpu.VMEM((CHUNKS, nz - 1, piece2 // down, D // across), BF16),
+            pltpu.VMEM((CHUNKS, CHUNK_ROWS, D), BF16),
             pltpu.SemaphoreType.DMA((n_off,)),
             pltpu.SemaphoreType.DMA((n_off,)),
             pltpu.SemaphoreType.DMA((n_off,)),
             pltpu.SemaphoreType.DMA((n_off,)),
-            pltpu.SemaphoreType.DMA((HEADS, n_sem)),
-            pltpu.SemaphoreType.DMA((HEADS, n_sem)),
-            pltpu.SemaphoreType.DMA((HEADS,)),
+            pltpu.SemaphoreType.DMA((CHUNKS, n_sem)),
+            pltpu.SemaphoreType.DMA((CHUNKS, n_sem)),
+            pltpu.SemaphoreType.DMA((CHUNKS,)),
+            pltpu.SemaphoreType.DMA((5,)),
         ],
         compiler_params=pltpu.CompilerParams(
-            collective_id=0, has_side_effects=True, vmem_limit_bytes=48 * 1024 * 1024
+            collective_id=0, has_side_effects=True, vmem_limit_bytes=60 * 1024 * 1024
         ),
         cost_estimate=pl.CostEstimate(
             flops=8 * 10**9, bytes_accessed=8 * 2**20, transcendentals=2 * 2**20
@@ -501,13 +567,27 @@
         name="layer",
     )(key_tiles, tile_valid, features, cotangent, weight_qkv, weight_out)
     factor = float(patches * nx * ROWS) ** (-0.5)
-    grad_qkv = gathered[:, :, : 3 * HW].reshape(HEADS, D, 3, HW).transpose(1, 2, 0, 3)
-    grad_out = gathered[:, :, 3 * HW :].reshape(HEADS, D // HW, HW, HW).transpose(0, 2, 1, 3)
-    return (
-        grad_features,
-        grad_qkv.reshape(D, 3 * D).astype(F32) * factor,
-        grad_out.reshape(D, D).astype(F32) * factor,
-    )
+    chunks = gathered.reshape(HEADS, D, D)
+    grad_qkv, grad_out, grad_features = pl.pallas_call(
+        functools.partial(finish, factor),
+        grid=(D // HW,),
+        out_shape=(
+            jax.ShapeDtypeStruct((D, 3 * D), F32),
+            jax.ShapeDtypeStruct((D, D), F32),
+            jax.ShapeDtypeStruct((1, ROWS, D), BF16),
+        ),
+        in_specs=[
+            pl.BlockSpec((HEADS, HW, D), lambda r: (0, r, 0)),
+            pl.BlockSpec((1, HW, D), lambda r: (0, r, 0)),
+        ],
+        out_specs=(
+            pl.BlockSpec((HW, 3 * D), lambda r: (r, 0)),
+            pl.BlockSpec((D, HW), lambda r: (0, r)),
+            pl.BlockSpec((1, HW, D), lambda r: (0, r, 0)),
+        ),
+        name="finish",
+    )(chunks, grad_features)
+    return grad_features, grad_qkv, grad_out
 
 
 def solution(mesh):

time: 140 us -> 98.1 us (0.70)
  Pallas kernels: 116 us -> 94.2 us
  local copies, waits for them, and re-layouts: 19.6 us -> 2.97 us
  other arithmetic: 2.04 us -> 0 us
    pallas_call x1, Pallas kernels: 116 us -> 89.7 us  [on_device(): pl.pallas_call(functools.partial(kernel, dims), out_shape=(jax.ShapeDtype...]
    unnamed x13 -> x2, local copies, waits for them, and re-layouts: 11.5 us -> 2.97 us
    mul x3 -> x0, local copies, waits for them, and re-layouts: 8.07 us -> none  [the longest x2 7.39 us: on_device(): grad_qkv.reshape(D, 3 * D).astype(F32) * factor]
    pallas_call x0 -> x1, Pallas kernels: none -> 4.49 us  [on_device(): pl.pallas_call(functools.partial(finish, factor), grid=(D // HW,), out_sh...]
    mul x2 -> x0, other arithmetic: 2.04 us -> none  [the longest x1 1.94 us: on_device(): grad_qkv.reshape(D, 3 * D).astype(F32) * factor]
where the time goes in v2:
time: 98.1 us; the launch traced here: 97.8 us
  Pallas kernels  94.2 us (96%)
  local copies, waits for them, and re-layouts  2.97 us (3%)
    pallas_call x1, Pallas kernels, on_device(): pl.pallas_call(functools.partial(kernel, dims), out_shape=(jax.ShapeDtype...  89.7 us
    pallas_call x1, Pallas kernels, on_device(): pl.pallas_call(functools.partial(finish, factor), grid=(D // HW,), out_sh...  4.49 us
    unnamed x2, local copies, waits for them, and re-layouts  2.97 us

profile of v2, /device:TPU:1, one launch (start us, length us, event | category | flops | bytes accessed | tf_op | source)
XLA Modules:
  0.0 97.8 jit_solution(14376159542187154073)
XLA Ops:
  0.6 1.5 %copy.9.kt = s32[256,8]{1,0:T(8,128)} copy(s32[256,8]{0,1:T(8,128)} %param.10) | data formatting | bytes 16384 | tf_op args[4]
  2.1 1.5 %copy.10.tv = s32[256,8]{1,0:T(8,128)} copy(s32[256,8]{0,1:T(8,128)} %param.11) | data formatting | bytes 16384 | tf_op args[5]
  3.6 89.7 %layer.1 = (bf16[1,512,512]{2,1,0:T(8,128)(2,1)}, bf16[1,2048,512]{2,1,0:T(8,128)(2,1)}) custom-call(s32[256,8]{1,0:T(8,128)} %copy.9.kt, s32[256,8]{1,0:T(8,128)} %copy.10.tv, bf16[1,512,512]{2,1,0:T(8,128)(2,1)} %x_hbm.1, bf16[1,512,512]{2,1,0:T(8,128)(2,1)} %c_hbm.1, bf16[512,1536]{1,0:T(8,128)(2,1)} %w_hbm.1, bf16[512,512]{1,0:T(8,128)(2,1)} %wo_hbm.1), custom_call_target="tpu_custom_call" | custom-call | flops 8000000000 | bytes 8388608 | tf_op jit(solution)/shard_map/layer/pallas_call | solution.py:512
  93.3 4.5 %finish.1 = (f32[512,1536]{1,0:T(8,128)}, f32[512,512]{1,0:T(8,128)}, bf16[1,512,512]{2,1,0:T(8,128)(2,1)}) custom-call(bf16[4,512,512]{2,1,0:T(8,128)(2,1)} %bitcast.1, bf16[1,512,512]{2,1,0:T(8,128)(2,1)} %get-tuple-element.9.features), custom_call_target="tpu_custom_call" | custom-call | tf_op jit(solution)/shard_map/finish/pallas_call | solution.py:571

commit v3 on v2

v3 whole, which is shorter than its diff:
```python
import functools

import jax
import jax.numpy as jnp
from jax import lax
from jax.experimental import pallas as pl
from jax.experimental.pallas import tpu as pltpu
from jax.sharding import PartitionSpec as P

HEADS = 4
TILE = 128
LOCAL = 4
REACH = 2
OFFSETS = [-2, -1, 1, 2]
CHIPS_Y = 4
EPS = 1e-06
MESH = pl.DeviceIdType.MESH
F32 = jnp.float32
BF16 = jnp.bfloat16
LOG2E = 1.4426950408889634
ROWS = LOCAL * TILE
HALO = 2 * TILE
ALL = ROWS + len(OFFSETS) * HALO
D = 512
HW = D // HEADS
HALF = D // 2


def nn(a, b):
    return lax.dot_general(a, b, (((1,), (0,)), ((), ())), preferred_element_type=F32)


def nt(a, b):
    return lax.dot_general(a, b, (((1,), (1,)), ((), ())), preferred_element_type=F32)


def tt(a, b):
    return lax.dot_general(a, b, (((0,), (1,)), ((), ())), preferred_element_type=F32)


def tn(a, b):
    return lax.dot_general(a, b, (((0,), (0,)), ((), ())), preferred_element_type=F32)


def normalise(rows):
    wide = rows.astype(F32)
    inverse = lax.rsqrt(jnp.mean(wide * wide, -1, keepdims=True) + EPS)
    return wide, inverse


def kernel(
    dims,
    kt_hbm,
    tv_hbm,
    x_hbm,
    c_hbm,
    w_hbm,
    wo_hbm,
    gf_hbm,
    out_ref,
    kt,
    tv,
    gf_ref,
    x_ref,
    c_ref,
    w_ref,
    wo_ref,
    stage,
    halo,
    normed_t,
    q,
    k,
    v,
    ga,
    q_t,
    ga_t,
    bias,
    own_scores,
    own_dprob,
    prob,
    dscore,
    attended,
    dquery,
    dkv_t,
    back_out,
    back_in,
    local,
    got0,
    sum0,
    got1,
    sum1,
    got2,
    sum2,
    got3,
    res,
    halo_send,
    halo_recv,
    back_send,
    back_recv,
    red_send,
    red_recv,
    out_sem,
    in_sem,
):
    patches, nz, ny, nx = dims
    p = lax.axis_index("patch")
    sx = lax.axis_index("sample")
    core = lax.rem(p, 2)
    y = lax.rem(lax.div(p, 2), ny)
    z = lax.div(p, 2 * ny)

    def patch_at(zz, yy):
        return (zz * ny + yy) * 2 + core

    def first(j):
        return (
            patch_at(z, lax.rem(y + j * core, ny)),
            lax.rem(sx + j * (1 - core), nx),
        )

    def second(j):
        return (
            patch_at(z, lax.rem(y + j * (1 - core), ny)),
            lax.rem(sx + j * core, nx),
        )

    def along_z(j):
        return (patch_at(lax.rem(z + j, nz), y), sx)

    pair = (p + 1 - 2 * core, sx)
    m1 = sx * (1 - core) + y * core
    m2 = sx * core + y * (1 - core)
    group = nx

    loads = [
        pltpu.make_async_copy(src, dst, in_sem.at[i])
        for i, (src, dst) in enumerate(
            (
                (x_hbm, x_ref),
                (w_hbm, w_ref),
                (c_hbm, c_ref),
                (wo_hbm, wo_ref),
                (kt_hbm, kt),
                (tv_hbm, tv),
            )
        )
    ]
    for i in (4, 0, 5, 1, 2, 3):
        loads[i].start()

    barrier = pltpu.get_barrier_semaphore()
    greeted = (
        [(lax.rem(p + o + patches, patches), sx) for o in OFFSETS]
        + [pair]
        + [first(j) for j in range(1, group)]
        + [second(j) for j in range(1, group)]
        + [along_z(j) for j in range(1, nz)]
    )
    for device in greeted:
        pl.semaphore_signal(barrier, inc=1, device_id=device, device_id_type=MESH)

    loads[0].wait()
    loads[4].wait()
    named = []
    for oi, o in enumerate(OFFSETS):
        row = lax.rem(p - o + patches, patches) * LOCAL
        one = kt[row, LOCAL + oi]
        two = one
        for r in range(1, LOCAL):
            entry = kt[row + r, LOCAL + oi]
            two = jnp.where(entry != one, entry, two)
        named.append((one - p * LOCAL, two - p * LOCAL))
        for s in range(2):
            tile = x_ref[0, 0:TILE, :]
            for r in range(1, LOCAL):
                tile = jnp.where(named[oi][s] == r, x_ref[0, r * TILE : (r + 1) * TILE, :], tile)
            stage[oi, s * TILE : (s + 1) * TILE, :] = tile

    pl.semaphore_wait(barrier, len(greeted))

    def halo_copy(oi, o=None):
        o = OFFSETS[oi] if o is None else o
        return pltpu.make_async_remote_copy(
            src_ref=stage.at[oi],
            dst_ref=halo.at[oi],
            send_sem=halo_send.at[oi],
            recv_sem=halo_recv.at[oi],
            device_id=(lax.rem(p - o + patches, patches), sx),
            device_id_type=MESH,
        )

    def back_copy(oi):
        return pltpu.make_async_remote_copy(
            src_ref=back_out.at[oi],
            dst_ref=back_in.at[oi],
            send_sem=back_send.at[oi],
            recv_sem=back_recv.at[oi],
            device_id=(lax.rem(p + OFFSETS[oi] + patches, patches), sx),
            device_id_type=MESH,
        )

    for oi in (0, 3, 1, 2):
        halo_copy(oi).start()

    loads[5].wait()
    base = p * LOCAL
    pick = []
    for t in range(LOCAL):
        pick.append(
            [
                jnp.where(kt[base + t, LOCAL + n] != kt[base, LOCAL + n], 1, 0)
                for n in range(len(OFFSETS))
            ]
        )
        for r in range(LOCAL):
            flag = jnp.int32(0)
            for j in range(LOCAL):
                flag = flag + jnp.where(kt[base + t, j] == base + r, tv[base + t, j], 0)
            low = jnp.where(flag > 0, jnp.float32(0.0), jnp.float32(-1e30))
            bias[t, :, r * TILE : (r + 1) * TILE] = jnp.full((8, TILE), low, F32)
        for n in range(len(OFFSETS)):
            flag = tv[base + t, LOCAL + n]
            low = jnp.where(flag > 0, jnp.float32(0.0), jnp.float32(-1e30))
            bias[t, :, ROWS + n * TILE : ROWS + (n + 1) * TILE] = jnp.full((8, TILE), low, F32)

    loads[1].wait()
    wide, inverse = normalise(x_ref[0])
    low = (wide * inverse).astype(BF16)
    normed_t[:, 0:ROWS] = low.T
    for part, target in ((0, q), (1, k), (2, v)):
        for half in range(2):
            at = part * D + half * 2 * HW
            got = nn(low, w_ref[:, at : at + 2 * HW]).astype(BF16)
            for i in range(2):
                piece = got[:, i * HW : (i + 1) * HW]
                target[half * 2 + i, 0:ROWS, :] = piece
                if part == 0:
                    q_t[half * 2 + i] = piece.T
    loads[2].wait()
    loads[3].wait()
    for half in range(2):
        at = half * 2 * HW
        got = nt(c_ref[0], wo_ref[at : at + 2 * HW, :]).astype(BF16)
        for i in range(2):
            piece = got[:, i * HW : (i + 1) * HW]
            ga[half * 2 + i] = piece
            ga_t[half * 2 + i] = piece.T

    for h in range(HEADS):
        own_scores[h] = nt(q[h], k[h, 0:ROWS, :])
        own_dprob[h] = nt(ga[h], v[h, 0:ROWS, :])

    for oi, o in ((2 - core, 1 - 2 * core), (1 + core, 2 * core - 1), (0, -2), (3, 2)):
        halo_copy(oi, o).wait_recv()
        wide, inverse = normalise(halo[oi])
        low = (wide * inverse).astype(BF16)
        at_row = pl.ds(pl.multiple_of(ROWS + oi * HALO, HALO), HALO)
        normed_t[:, at_row] = low.T
        for part, target in ((1, k), (2, v)):
            for half in range(2):
                at = part * D + half * 2 * HW
                got = nn(low, w_ref[:, at : at + 2 * HW]).astype(BF16)
                for i in range(2):
                    target[half * 2 + i, at_row, :] = got[:, i * HW : (i + 1) * HW]

    n1 = group - 1
    piece1 = HALF // group
    per_owner = HEADS // group
    piece2 = per_owner * piece1
    down, across = split_last(piece2, nz)
    piece3, width3 = piece2 // down, D // across
    half_at = core * HALF
    at1 = half_at + m1 * piece1
    counts = reduction_counts(group, nz)
    firsts = [sum(counts[:i]) for i in range(len(counts))]

    def rows_at(start, size):
        return pl.ds(pl.multiple_of(start, 16), size)

    def owned(owner):
        return pl.ds(owner * per_owner, per_owner)

    def last_piece(index):
        return (
            rows_at(lax.div(index, across) * piece3, piece3),
            pl.ds(pl.multiple_of(lax.rem(index, across) * width3, 128), width3),
        )

    def last_place(index):
        row = lax.div(index, across) * piece3
        head_at = m2 * per_owner + lax.div(row, piece1)
        rows = rows_at(at1 + lax.rem(row, piece1), piece3)
        return head_at, rows, last_piece(index)[1]

    def move(phase, i, src, dst, device):
        return pltpu.make_async_remote_copy(
            src_ref=src,
            dst_ref=dst,
            send_sem=red_send.at[firsts[phase] + i],
            recv_sem=red_recv.at[firsts[phase] + i],
            device_id=device,
            device_id_type=MESH,
        )

    def to_pair(h):
        src = local.at[h, rows_at((1 - core) * HALF, HALF), :]
        return [move(0, h, src, got0.at[h], pair)]

    def scatter_first(h):
        return [
            move(
                1,
                h * n1 + j - 1,
                sum0.at[h, rows_at(lax.rem(m1 + j, group) * piece1, piece1), :],
                got1.at[h, j - 1],
                first(j),
            )
            for j in range(1, group)
        ]

    def scatter_second():
        return [
            move(
                2,
                j - 1,
                sum1.at[rows_at(lax.rem(m2 + j, group) * piece2, piece2), :],
                got2.at[j - 1],
                second(j),
            )
            for j in range(1, group)
        ]

    def scatter_z():
        moves = []
        for j in range(1, nz):
            rows, columns = last_piece(lax.rem(z + j, nz))
            moves.append(move(3, j - 1, sum2.at[rows, columns], got3.at[j - 1], along_z(j)))
        return moves

    def gather_z():
        mine = res.at[last_place(z)]
        return [move(4, j - 1, mine, mine, along_z(j)) for j in range(1, nz)]

    def gather_second():
        mine = res.at[owned(m2), rows_at(at1, piece1), :]
        return [move(5, j - 1, mine, mine, second(j)) for j in range(1, group)]

    def gather_first(i):
        mine = res.at[owned(lax.rem(m2 - i + group, group)), rows_at(at1, piece1), :]
        return [move(6, i * n1 + j - 1, mine, mine, first(j)) for j in range(1, group)]

    def gather_pair(i):
        mine = res.at[owned(lax.rem(m2 - i + group, group)), rows_at(half_at, HALF), :]
        return [move(7, i, mine, mine, pair)]

    def start(copies):
        for copy in copies:
            copy.start()

    def arrive(copies):
        for copy in copies:
            copy.wait_recv()

    def add_pair(h):
        arrive(to_pair(h))
        mine = local[h, rows_at(half_at, HALF), :].astype(F32)
        sum0[h] = (mine + got0[h].astype(F32)).astype(BF16)
        start(scatter_first(h))

    def add_first(h):
        arrive(scatter_first(h))
        total = sum0[h, rows_at(m1 * piece1, piece1), :].astype(F32)
        for j in range(n1):
            total = total + got1[h, j].astype(F32)
        sum1[h * piece1 : (h + 1) * piece1, :] = total.astype(BF16)

    def add_second():
        arrive(scatter_second())
        total = sum1[rows_at(m2 * piece2, piece2), :].astype(F32)
        for j in range(n1):
            total = total + got2[j].astype(F32)
        sum2[...] = total.astype(BF16)
        start(scatter_z())

    def add_z():
        arrive(scatter_z())
        total = sum2[last_piece(z)].astype(F32)
        for j in range(nz - 1):
            total = total + got3[j].astype(F32)
        res[last_place(z)] = total.astype(BF16)
        start(gather_z())

    scaling = HW ** (-0.5)

    def head(h, carry):
        for t in range(LOCAL):
            rows = slice(t * TILE, (t + 1) * TILE)

            def chosen(ref):
                parts = [ref[h, 0:ROWS, :]]
                for n in range(len(OFFSETS)):
                    at = ROWS + n * HALO
                    near = ref[h, at : at + TILE, :]
                    far = ref[h, at + TILE : at + HALO, :]
                    parts.append(jnp.where(pick[t][n] == 0, near, far))
                return jnp.concatenate(parts, 0)

            keys = chosen(k)
            values = chosen(v)
            scores = jnp.concatenate(
                [own_scores[h, rows, :], nt(q[h, rows, :], keys[ROWS:])], 1
            )
            scores = scores + bias[t, 0:1, :]
            highest = jnp.max(scores, -1, keepdims=True)
            expanded = jnp.exp2((scores - highest) * (scaling * LOG2E))
            attention = expanded * (1.0 / jnp.sum(expanded, -1, keepdims=True))
            attention_low = attention.astype(BF16)
            dprob = jnp.concatenate(
                [own_dprob[h, rows, :], nt(ga[h, rows, :], values[ROWS:])], 1
            )
            centre = jnp.sum(attention * dprob, -1, keepdims=True)
            ds = (attention * (dprob - centre) * scaling).astype(BF16)
            attended[h, rows, :] = nn(attention_low, values).astype(BF16)
            dquery[h, rows, :] = nn(ds, keys).astype(BF16)
            for full, piece in ((prob, attention_low), (dscore, ds)):
                full[rows, 0:ROWS] = piece[:, 0:ROWS]
                for n in range(len(OFFSETS)):
                    part = piece[:, ROWS + n * TILE : ROWS + (n + 1) * TILE]
                    for s in range(2):
                        at = ROWS + (2 * n + s) * TILE
                        keep = jnp.where(pick[t][n] == s, 1.0, 0.0).astype(BF16)
                        full[rows, at : at + TILE] = part * keep

            if t == 2:

                @pl.when(h >= 1)
                def _():
                    add_pair(h - 1)

        at = pl.multiple_of(h * HW, HW)
        dk = nn(q_t[h], dscore[...]).astype(BF16)
        dv = nn(ga_t[h], prob[...]).astype(BF16)
        dkv_t[pl.ds(at, HW), :] = dk
        dkv_t[pl.ds(pl.multiple_of(D + h * HW, HW), HW), :] = dv
        local[h, :, 0:HW] = nn(normed_t[:, 0:ROWS], dquery[h]).astype(BF16)
        local[h, :, HW : 2 * HW] = nt(normed_t[...], dk).astype(BF16)
        local[h, :, 2 * HW : 3 * HW] = nt(normed_t[...], dv).astype(BF16)
        outer = tn(attended[h], c_ref[0]).astype(BF16)
        for r in range(D // HW):
            local[h, r * HW : (r + 1) * HW, 3 * HW :] = outer[:, r * HW : (r + 1) * HW]
        start(to_pair(h))
        return carry

    lax.fori_loop(0, HEADS, head, 0)

    def give_back(oi):
        at = ROWS + oi * HALO
        back_out[oi] = tt(dkv_t[:, at : at + HALO], w_ref[:, D:]).astype(BF16)
        back_copy(oi).start()

    def own_grad():
        total = tt(dkv_t[:, 0:ROWS], w_ref[:, D:])
        for h in range(HEADS):
            total = total + nt(dquery[h], w_ref[:, h * HW : (h + 1) * HW])
        return total

    def finish_features(grad):
        for oi in range(len(OFFSETS)):
            back_copy(oi).wait_recv()
        for r in range(LOCAL):
            rows = slice(r * TILE, (r + 1) * TILE)
            total = grad[rows]
            for oi in range(len(OFFSETS)):
                for s in range(2):
                    came = back_in[oi, s * TILE : (s + 1) * TILE, :].astype(F32)
                    total = total + jnp.where(named[oi][s] == r, came, 0.0)
            wide, inverse = normalise(x_ref[0, rows, :])
            normed = wide * inverse
            mean = jnp.mean(total * normed, -1, keepdims=True)
            result = c_ref[0, rows, :].astype(F32) + inverse * (total - normed * mean)
            gf_ref[0, rows, :] = result.astype(BF16)
        features_copy.start()

    out_copy = pltpu.make_async_copy(res, out_ref, out_sem)
    features_copy = pltpu.make_async_copy(gf_ref, gf_hbm, in_sem.at[6])
    give_back(0)
    give_back(3)
    add_pair(HEADS - 1)
    give_back(1)
    give_back(2)
    for h in range(HEADS):
        add_first(h)
    start(scatter_second())
    grad = own_grad()
    add_second()
    add_z()
    finish_features(grad)
    arrive(gather_z())
    start(gather_second())
    start(gather_first(0))
    for j in range(1, group):
        arrive(gather_second()[j - 1 : j])
        start(gather_first(j))
    for i in range(group):
        arrive(gather_first(i))
        start(gather_pair(i))
    for i in range(group):
        arrive(gather_pair(i))
    out_copy.start()
    for oi in range(len(OFFSETS)):
        halo_copy(oi).wait_send()
        back_copy(oi).wait_send()

    def settle(h, carry):
        for copy in to_pair(h) + scatter_first(h):
            copy.wait_send()
        return carry

    lax.fori_loop(0, HEADS, settle, 0)
    for copy in scatter_second() + scatter_z() + gather_z() + gather_second():
        copy.wait_send()
    for i in range(group):
        for copy in gather_first(i) + gather_pair(i):
            copy.wait_send()
    out_copy.wait()
    features_copy.wait()


def reduction_counts(group, nz):
    n1 = group - 1
    return [HEADS, HEADS * n1, n1, nz - 1, nz - 1, n1, group * n1, group]


def split_last(rows, count):
    down = min(count, rows // 16)
    return down, count // down


def finish(factor, chunks, features, qkv, out, grad_features):
    for h in range(HEADS):
        for part in range(3):
            piece = chunks[h, :, part * HW : (part + 1) * HW]
            at = part * D + h * HW
            qkv[:, at : at + HW] = piece.astype(F32) * factor
        out[h * HW : (h + 1) * HW, :] = chunks[h, :, 3 * HW :].astype(F32) * factor
    grad_features[...] = features[...]


def on_device(dims, features, cotangent, weight_qkv, weight_out, key_tiles, tile_valid):
    patches, nz, ny, nx = dims
    group = nx
    piece1 = HALF // group
    piece2 = HEADS // group * piece1
    down, across = split_last(piece2, nz)
    n_sem = sum(reduction_counts(group, nz))
    n_off = len(OFFSETS)
    grad_features, gathered = pl.pallas_call(
        functools.partial(kernel, dims),
        out_shape=(
            jax.ShapeDtypeStruct((1, ROWS, D), BF16),
            jax.ShapeDtypeStruct((HEADS, D, D), BF16),
        ),
        in_specs=[pl.BlockSpec(memory_space=pltpu.HBM)] * 6,
        out_specs=(pl.BlockSpec(memory_space=pl.ANY), pl.BlockSpec(memory_space=pl.ANY)),
        scratch_shapes=[
            pltpu.SMEM(key_tiles.shape, jnp.int32),
            pltpu.SMEM(tile_valid.shape, jnp.int32),
            pltpu.VMEM((1, ROWS, D), BF16),
            pltpu.VMEM((1, ROWS, D), BF16),
            pltpu.VMEM((1, ROWS, D), BF16),
            pltpu.VMEM((D, 3 * D), BF16),
            pltpu.VMEM((D, D), BF16),
            pltpu.VMEM((n_off, HALO, D), BF16),
            pltpu.VMEM((n_off, HALO, D), BF16),
            pltpu.VMEM((D, ALL), BF16),
            pltpu.VMEM((HEADS, ROWS, HW), BF16),
            pltpu.VMEM((HEADS, ALL, HW), BF16),
            pltpu.VMEM((HEADS, ALL, HW), BF16),
            pltpu.VMEM((HEADS, ROWS, HW), BF16),
            pltpu.VMEM((HEADS, HW, ROWS), BF16),
            pltpu.VMEM((HEADS, HW, ROWS), BF16),
            pltpu.VMEM((LOCAL, 8, 2 * ROWS), F32),
            pltpu.VMEM((HEADS, ROWS, ROWS), F32),
            pltpu.VMEM((HEADS, ROWS, ROWS), F32),
            pltpu.VMEM((ROWS, ALL), BF16),
            pltpu.VMEM((ROWS, ALL), BF16),
            pltpu.VMEM((HEADS, ROWS, HW), BF16),
            pltpu.VMEM((HEADS, ROWS, HW), BF16),
            pltpu.VMEM((2 * D, ALL), BF16),
            pltpu.VMEM((n_off, HALO, D), BF16),
            pltpu.VMEM((n_off, HALO, D), BF16),
            pltpu.VMEM((HEADS, D, D), BF16),
            pltpu.VMEM((HEADS, HALF, D), BF16),
            pltpu.VMEM((HEADS, HALF, D), BF16),
            pltpu.VMEM((HEADS, group - 1, piece1, D), BF16),
            pltpu.VMEM((HEADS * piece1, D), BF16),
            pltpu.VMEM((group - 1, piece2, D), BF16),
            pltpu.VMEM((piece2, D), BF16),
            pltpu.VMEM((nz - 1, piece2 // down, D // across), BF16),
            pltpu.VMEM((HEADS, D, D), BF16),
            pltpu.SemaphoreType.DMA((n_off,)),
            pltpu.SemaphoreType.DMA((n_off,)),
            pltpu.SemaphoreType.DMA((n_off,)),
            pltpu.SemaphoreType.DMA((n_off,)),
            pltpu.SemaphoreType.DMA((n_sem,)),
            pltpu.SemaphoreType.DMA((n_sem,)),
            pltpu.SemaphoreType.DMA,
            pltpu.SemaphoreType.DMA((7,)),
        ],
        compiler_params=pltpu.CompilerParams(
            collective_id=0, has_side_effects=True, vmem_limit_bytes=60 * 1024 * 1024
        ),
        cost_estimate=pl.CostEstimate(
            flops=8 * 10**9, bytes_accessed=8 * 2**20, transcendentals=2 * 2**20
        ),
        name="layer",
    )(key_tiles, tile_valid, features, cotangent, weight_qkv, weight_out)
    factor = float(patches * nx * ROWS) ** (-0.5)
    grad_qkv, grad_out, grad_features = pl.pallas_call(
        functools.partial(finish, factor),
        grid=(D // HW,),
        out_shape=(
            jax.ShapeDtypeStruct((D, 3 * D), F32),
            jax.ShapeDtypeStruct((D, D), F32),
            jax.ShapeDtypeStruct((1, ROWS, D), BF16),
        ),
        in_specs=[
            pl.BlockSpec((HEADS, HW, D), lambda r: (0, r, 0)),
            pl.BlockSpec((1, HW, D), lambda r: (0, r, 0)),
        ],
        out_specs=(
            pl.BlockSpec((HW, 3 * D), lambda r: (r, 0)),
            pl.BlockSpec((D, HW), lambda r: (0, r)),
            pl.BlockSpec((1, HW, D), lambda r: (0, r, 0)),
        ),
        name="finish",
    )(gathered, grad_features)
    return grad_features, grad_qkv, grad_out


def solution(mesh):
    patches = mesh.shape["patch"]
    dims = (patches, patches // (2 * CHIPS_Y), CHIPS_Y, mesh.shape["sample"])
    placed = (P("sample", "patch", None), P("sample", "patch", None), P(), P(), P(), P())
    return jax.shard_map(
        functools.partial(on_device, dims),
        mesh=mesh,
        in_specs=placed,
        out_specs=(P("sample", "patch", None), P(), P()),
        check_vma=False,
    )
```

time: 98.1 us -> 89.1 us (0.908)
  Pallas kernels: 94.2 us -> 85.3 us
    pallas_call x1, Pallas kernels: 89.7 us -> 80.8 us  [on_device(): pl.pallas_call(functools.partial(kernel, dims), out_shape=(jax.ShapeDtype...]
where the time goes in v3:
time: 89.1 us; the launch traced here: 88.9 us
  Pallas kernels  85.3 us (96%)
  local copies, waits for them, and re-layouts  2.97 us (3%)
    pallas_call x1, Pallas kernels, on_device(): pl.pallas_call(functools.partial(kernel, dims), out_shape=(jax.ShapeDtype...  80.8 us
    pallas_call x1, Pallas kernels, on_device(): pl.pallas_call(functools.partial(finish, factor), grid=(D // HW,), out_sh...  4.49 us
    unnamed x2, local copies, waits for them, and re-layouts  2.97 us

profile of v3, /device:TPU:1, one launch (start us, length us, event | category | flops | bytes accessed | tf_op | source)
XLA Modules:
  0.0 88.9 jit_solution(18396882835610091441)
XLA Ops:
  0.6 1.5 %copy.9.kt_hbm = s32[256,8]{1,0:T(8,128)} copy(s32[256,8]{0,1:T(8,128)} %param.10) | data formatting | bytes 16384 | tf_op args[4]
  2.1 1.5 %copy.10.tv_hbm = s32[256,8]{1,0:T(8,128)} copy(s32[256,8]{0,1:T(8,128)} %param.11) | data formatting | bytes 16384 | tf_op args[5]
  3.6 80.8 %layer.1 = (bf16[1,512,512]{2,1,0:T(8,128)(2,1)}, bf16[4,512,512]{2,1,0:T(8,128)(2,1)}) custom-call(s32[256,8]{1,0:T(8,128)} %copy.9.kt_hbm, s32[256,8]{1,0:T(8,128)} %copy.10.tv_hbm, bf16[1,512,512]{2,1,0:T(8,128)(2,1)} %x_hbm.1, bf16[1,512,512]{2,1,0:T(8,128)(2,1)} %c_hbm.1, bf16[512,1536]{1,0:T(8,128)(2,1)} %w_hbm.1, bf16[512,512]{1,0:T(8,128)(2,1)} %wo_hbm.1), custom_call_target="tpu_custom_call" | custom-call | flops 8000000000 | bytes 8388608 | tf_op jit(solution)/shard_map/layer/pallas_call | solution.py:557
  84.4 4.5 %finish.1 = (f32[512,1536]{1,0:T(8,128)}, f32[512,512]{1,0:T(8,128)}, bf16[1,512,512]{2,1,0:T(8,128)(2,1)}) custom-call(bf16[4,512,512]{2,1,0:T(8,128)(2,1)} %get-tuple-element.8.chunks, bf16[1,512,512]{2,1,0:T(8,128)(2,1)} %get-tuple-element.9.features), custom_call_target="tpu_custom_call" | custom-call | tf_op jit(solution)/shard_map/finish/pallas_call | solution.py:619

commit v4 on v3

--- a/solution.py
+++ b/solution.py
@@ -164,10 +164,10 @@
     named = []
     for oi, o in enumerate(OFFSETS):
         row = lax.rem(p - o + patches, patches) * LOCAL
-        one = kt[row, LOCAL + oi]
+        one = kt[LOCAL + oi, row]
         two = one
         for r in range(1, LOCAL):
-            entry = kt[row + r, LOCAL + oi]
+            entry = kt[LOCAL + oi, row + r]
             two = jnp.where(entry != one, entry, two)
         named.append((one - p * LOCAL, two - p * LOCAL))
         for s in range(2):
@@ -208,18 +208,18 @@
     for t in range(LOCAL):
         pick.append(
             [
-                jnp.where(kt[base + t, LOCAL + n] != kt[base, LOCAL + n], 1, 0)
+                jnp.where(kt[LOCAL + n, base + t] != kt[LOCAL + n, base], 1, 0)
                 for n in range(len(OFFSETS))
             ]
         )
         for r in range(LOCAL):
             flag = jnp.int32(0)
             for j in range(LOCAL):
-                flag = flag + jnp.where(kt[base + t, j] == base + r, tv[base + t, j], 0)
+                flag = flag + jnp.where(kt[j, base + t] == base + r, tv[j, base + t], 0)
             low = jnp.where(flag > 0, jnp.float32(0.0), jnp.float32(-1e30))
             bias[t, :, r * TILE : (r + 1) * TILE] = jnp.full((8, TILE), low, F32)
         for n in range(len(OFFSETS)):
-            flag = tv[base + t, LOCAL + n]
+            flag = tv[LOCAL + n, base + t]
             low = jnp.where(flag > 0, jnp.float32(0.0), jnp.float32(-1e30))
             bias[t, :, ROWS + n * TILE : ROWS + (n + 1) * TILE] = jnp.full((8, TILE), low, F32)
 
@@ -443,8 +443,8 @@
         dkv_t[pl.ds(at, HW), :] = dk
         dkv_t[pl.ds(pl.multiple_of(D + h * HW, HW), HW), :] = dv
         local[h, :, 0:HW] = nn(normed_t[:, 0:ROWS], dquery[h]).astype(BF16)
-        local[h, :, HW : 2 * HW] = nt(normed_t[...], dk).astype(BF16)
-        local[h, :, 2 * HW : 3 * HW] = nt(normed_t[...], dv).astype(BF16)
+        both = jnp.concatenate([dk, dv], 0)
+        local[h, :, HW : 3 * HW] = nt(normed_t[...], both).astype(BF16)
         outer = tn(attended[h], c_ref[0]).astype(BF16)
         for r in range(D // HW):
             local[h, r * HW : (r + 1) * HW, 3 * HW :] = outer[:, r * HW : (r + 1) * HW]
@@ -456,7 +456,6 @@
     def give_back(oi):
         at = ROWS + oi * HALO
         back_out[oi] = tt(dkv_t[:, at : at + HALO], w_ref[:, D:]).astype(BF16)
-        back_copy(oi).start()
 
     def own_grad():
         total = tt(dkv_t[:, 0:ROWS], w_ref[:, D:])
@@ -481,7 +480,10 @@
             gf_ref[0, rows, :] = result.astype(BF16)
         features_copy.start()
 
-    out_copy = pltpu.make_async_copy(res, out_ref, out_sem)
+    def out_copy(index, owner, row):
+        piece = (owned(lax.rem(owner - index + 2 * group, group)), rows_at(row, HALF), slice(None))
+        return pltpu.make_async_copy(res.at[piece], out_ref.at[piece], out_sem.at[index])
+
     features_copy = pltpu.make_async_copy(gf_ref, gf_hbm, in_sem.at[6])
     give_back(0)
     give_back(3)
@@ -493,20 +495,23 @@
     start(scatter_second())
     grad = own_grad()
     add_second()
+    for oi in (0, 3, 1, 2):
+        back_copy(oi).start()
     add_z()
-    finish_features(grad)
     arrive(gather_z())
     start(gather_second())
     start(gather_first(0))
     for j in range(1, group):
         arrive(gather_second()[j - 1 : j])
         start(gather_first(j))
+    finish_features(grad)
     for i in range(group):
         arrive(gather_first(i))
         start(gather_pair(i))
+        out_copy(i, m2, half_at).start()
     for i in range(group):
         arrive(gather_pair(i))
-    out_copy.start()
+        out_copy(group + i, m1, HALF - half_at).start()
     for oi in range(len(OFFSETS)):
         halo_copy(oi).wait_send()
         back_copy(oi).wait_send()
@@ -522,7 +527,9 @@
     for i in range(group):
         for copy in gather_first(i) + gather_pair(i):
             copy.wait_send()
-    out_copy.wait()
+    for i in range(group):
+        out_copy(i, m2, half_at).wait()
+        out_copy(group + i, m1, HALF - half_at).wait()
     features_copy.wait()
 
 
@@ -542,7 +549,8 @@
             piece = chunks[h, :, part * HW : (part + 1) * HW]
             at = part * D + h * HW
             qkv[:, at : at + HW] = piece.astype(F32) * factor
-        out[h * HW : (h + 1) * HW, :] = chunks[h, :, 3 * HW :].astype(F32) * factor
+        column = pl.ds(pl.multiple_of(pl.program_id(0) * HW, HW), HW)
+        out[h * HW : (h + 1) * HW, column] = chunks[h, :, 3 * HW :].astype(F32) * factor
     grad_features[...] = features[...]
 
 
@@ -563,8 +571,8 @@
         in_specs=[pl.BlockSpec(memory_space=pltpu.HBM)] * 6,
         out_specs=(pl.BlockSpec(memory_space=pl.ANY), pl.BlockSpec(memory_space=pl.ANY)),
         scratch_shapes=[
-            pltpu.SMEM(key_tiles.shape, jnp.int32),
-            pltpu.SMEM(tile_valid.shape, jnp.int32),
+            pltpu.SMEM(key_tiles.shape[::-1], jnp.int32),
+            pltpu.SMEM(tile_valid.shape[::-1], jnp.int32),
             pltpu.VMEM((1, ROWS, D), BF16),
             pltpu.VMEM((1, ROWS, D), BF16),
             pltpu.VMEM((1, ROWS, D), BF16),
@@ -604,7 +612,7 @@
             pltpu.SemaphoreType.DMA((n_off,)),
             pltpu.SemaphoreType.DMA((n_sem,)),
             pltpu.SemaphoreType.DMA((n_sem,)),
-            pltpu.SemaphoreType.DMA,
+            pltpu.SemaphoreType.DMA((2 * group,)),
             pltpu.SemaphoreType.DMA((7,)),
         ],
         compiler_params=pltpu.CompilerParams(
@@ -614,7 +622,7 @@
             flops=8 * 10**9, bytes_accessed=8 * 2**20, transcendentals=2 * 2**20
         ),
         name="layer",
-    )(key_tiles, tile_valid, features, cotangent, weight_qkv, weight_out)
+    )(key_tiles.T, tile_valid.T, features, cotangent, weight_qkv, weight_out)
     factor = float(patches * nx * ROWS) ** (-0.5)
     grad_qkv, grad_out, grad_features = pl.pallas_call(
         functools.partial(finish, factor),
@@ -630,7 +638,7 @@
         ],
         out_specs=(
             pl.BlockSpec((HW, 3 * D), lambda r: (r, 0)),
-            pl.BlockSpec((D, HW), lambda r: (0, r)),
+            pl.BlockSpec((D, D), lambda r: (0, 0)),
             pl.BlockSpec((1, HW, D), lambda r: (0, r, 0)),
         ),
         name="finish",

time: 89.1 us -> 82.4 us (0.925)
  Pallas kernels: 85.3 us -> 81.6 us
  local copies, waits for them, and re-layouts: 2.97 us -> 0 us
    pallas_call x1, Pallas kernels: 80.8 us -> 76.9 us  [on_device(): pl.pallas_call(functools.partial(kernel, dims), out_shape=(jax.ShapeDtype...]
    unnamed x2 -> x0, local copies, waits for them, and re-layouts: 2.97 us -> none
where the time goes in v4:
time: 82.4 us; the launch traced here: 82.2 us
  Pallas kernels  81.6 us (99%)
    pallas_call x1, Pallas kernels, on_device(): pl.pallas_call(functools.partial(kernel, dims), out_shape=(jax.ShapeDtype...  76.9 us
    pallas_call x1, Pallas kernels, on_device(): pl.pallas_call(functools.partial(finish, factor), grid=(D // HW,), out_sh...  4.62 us

profile of v4, /device:TPU:1, one launch (start us, length us, event | category | flops | bytes accessed | tf_op | source)
XLA Modules:
  0.0 82.2 jit_solution(1887857334179962023)
XLA Ops:
  0.6 76.9 %layer.1 = (bf16[1,512,512]{2,1,0:T(8,128)(2,1)}, bf16[4,512,512]{2,1,0:T(8,128)(2,1)}) custom-call(s32[8,256]{1,0:T(8,128)} %bitcast.2, s32[8,256]{1,0:T(8,128)} %bitcast.3, bf16[1,512,512]{2,1,0:T(8,128)(2,1)} %x_hbm.1, bf16[1,512,512]{2,1,0:T(8,128)(2,1)} %c_hbm.1, bf16[512,1536]{1,0:T(8,128)(2,1)} %w_hbm.1, bf16[512,512]{1,0:T(8,128)(2,1)} %wo_hbm.1), custom_call_target="tpu_custom_call" | custom-call | flops 8000000000 | bytes 8388608 | tf_op jit(solution)/shard_map/layer/pallas_call | solution.py:565
  77.6 4.6 %finish.1 = (f32[512,1536]{1,0:T(8,128)}, f32[512,512]{1,0:T(8,128)}, bf16[1,512,512]{2,1,0:T(8,128)(2,1)}) custom-call(bf16[4,512,512]{2,1,0:T(8,128)(2,1)} %get-tuple-element.8.chunks, bf16[1,512,512]{2,1,0:T(8,128)(2,1)} %get-tuple-element.9.features), custom_call_target="tpu_custom_call" | custom-call | tf_op jit(solution)/shard_map/finish/pallas_call | solution.py:627

commit v5 on v4

--- a/solution.py
+++ b/solution.py
@@ -486,14 +486,13 @@
 
     features_copy = pltpu.make_async_copy(gf_ref, gf_hbm, in_sem.at[6])
     give_back(0)
-    give_back(3)
     add_pair(HEADS - 1)
     give_back(1)
     give_back(2)
     for h in range(HEADS):
         add_first(h)
     start(scatter_second())
-    grad = own_grad()
+    give_back(3)
     add_second()
     for oi in (0, 3, 1, 2):
         back_copy(oi).start()
@@ -504,14 +503,12 @@
     for j in range(1, group):
         arrive(gather_second()[j - 1 : j])
         start(gather_first(j))
-    finish_features(grad)
+    grad = own_grad()
     for i in range(group):
         arrive(gather_first(i))
         start(gather_pair(i))
         out_copy(i, m2, half_at).start()
-    for i in range(group):
-        arrive(gather_pair(i))
-        out_copy(group + i, m1, HALF - half_at).start()
+    finish_features(grad)
     for oi in range(len(OFFSETS)):
         halo_copy(oi).wait_send()
         back_copy(oi).wait_send()
@@ -525,9 +522,14 @@
     for copy in scatter_second() + scatter_z() + gather_z() + gather_second():
         copy.wait_send()
     for i in range(group):
-        for copy in gather_first(i) + gather_pair(i):
+        for copy in gather_first(i):
             copy.wait_send()
     for i in range(group):
+        arrive(gather_pair(i))
+        out_copy(group + i, m1, HALF - half_at).start()
+    for i in range(group):
+        for copy in gather_pair(i):
+            copy.wait_send()
         out_copy(i, m2, half_at).wait()
         out_copy(group + i, m1, HALF - half_at).wait()
     features_copy.wait()
@@ -543,15 +545,36 @@
     return down, count // down
 
 
-def finish(factor, chunks, features, qkv, out, grad_features):
-    for h in range(HEADS):
-        for part in range(3):
-            piece = chunks[h, :, part * HW : (part + 1) * HW]
-            at = part * D + h * HW
-            qkv[:, at : at + HW] = piece.astype(F32) * factor
-        column = pl.ds(pl.multiple_of(pl.program_id(0) * HW, HW), HW)
-        out[h * HW : (h + 1) * HW, column] = chunks[h, :, 3 * HW :].astype(F32) * factor
-    grad_features[...] = features[...]
+def finish(factor, chunks, features, qkv, out, grad_features, low, wide, wide_out, held, sem_in, sem_out):
+    taken = pltpu.make_async_copy(features, held, sem_in.at[LOCAL])
+    passed = pltpu.make_async_copy(held, grad_features, sem_out.at[LOCAL + 1])
+    loads = []
+    for r in range(LOCAL):
+        rows = pl.ds(r * HW, HW)
+        loads.append(pltpu.make_async_copy(chunks.at[:, rows, :], low.at[r], sem_in.at[r]))
+        loads[r].start()
+    taken.start()
+    stores = []
+    for r in range(LOCAL):
+        loads[r].wait()
+        for h in range(HEADS):
+            for part in range(3):
+                piece = low[r, h, :, part * HW : (part + 1) * HW]
+                at = part * D + h * HW
+                wide[r, :, at : at + HW] = piece.astype(F32) * factor
+            piece = low[r, h, :, 3 * HW :].astype(F32) * factor
+            wide_out[h * HW : (h + 1) * HW, r * HW : (r + 1) * HW] = piece
+        stores.append(
+            pltpu.make_async_copy(wide.at[r], qkv.at[pl.ds(r * HW, HW), :], sem_out.at[r])
+        )
+        stores[r].start()
+    stores.append(pltpu.make_async_copy(wide_out, out, sem_out.at[LOCAL]))
+    stores[LOCAL].start()
+    taken.wait()
+    passed.start()
+    for store in stores:
+        store.wait()
+    passed.wait()
 
 
 def on_device(dims, features, cotangent, weight_qkv, weight_out, key_tiles, tile_valid):
@@ -626,21 +649,22 @@
     factor = float(patches * nx * ROWS) ** (-0.5)
     grad_qkv, grad_out, grad_features = pl.pallas_call(
         functools.partial(finish, factor),
-        grid=(D // HW,),
         out_shape=(
             jax.ShapeDtypeStruct((D, 3 * D), F32),
             jax.ShapeDtypeStruct((D, D), F32),
             jax.ShapeDtypeStruct((1, ROWS, D), BF16),
         ),
-        in_specs=[
-            pl.BlockSpec((HEADS, HW, D), lambda r: (0, r, 0)),
-            pl.BlockSpec((1, HW, D), lambda r: (0, r, 0)),
+        in_specs=[pl.BlockSpec(memory_space=pl.ANY)] * 2,
+        out_specs=(pl.BlockSpec(memory_space=pl.ANY),) * 3,
+        scratch_shapes=[
+            pltpu.VMEM((LOCAL, HEADS, HW, D), BF16),
+            pltpu.VMEM((LOCAL, HW, 3 * D), F32),
+            pltpu.VMEM((D, D), F32),
+            pltpu.VMEM((1, ROWS, D), BF16),
+            pltpu.SemaphoreType.DMA((LOCAL + 1,)),
+            pltpu.SemaphoreType.DMA((LOCAL + 2,)),
         ],
-        out_specs=(
-            pl.BlockSpec((HW, 3 * D), lambda r: (r, 0)),
-            pl.BlockSpec((D, D), lambda r: (0, 0)),
-            pl.BlockSpec((1, HW, D), lambda r: (0, r, 0)),
-        ),
+        compiler_params=pltpu.CompilerParams(vmem_limit_bytes=60 * 1024 * 1024),
         name="finish",
     )(gathered, grad_features)
     return grad_features, grad_qkv, grad_out

time: 82.4 us -> 81.6 us (level)
  Pallas kernels: 81.6 us -> 80.6 us
    pallas_call x1, Pallas kernels: 4.62 us -> 3.42 us  [on_device(): pl.pallas_call(functools.partial(finish, factor), out_shape=(jax.ShapeDty...]
where the time goes in v5:
time: 81.6 us; the launch traced here: 81.5 us
  Pallas kernels  80.6 us (99%)
    pallas_call x1, Pallas kernels, on_device(): pl.pallas_call(functools.partial(kernel, dims), out_shape=(jax.ShapeDtype...  77.2 us
    pallas_call x1, Pallas kernels, on_device(): pl.pallas_call(functools.partial(finish, factor), out_shape=(jax.ShapeDty...  3.42 us

profile of v5, /device:TPU:1, one launch (start us, length us, event | category | flops | bytes accessed | tf_op | source)
XLA Modules:
  0.0 81.5 jit_solution(9358286876878587236)
XLA Ops:
  0.6 77.2 %layer.1 = (bf16[1,512,512]{2,1,0:T(8,128)(2,1)}, bf16[4,512,512]{2,1,0:T(8,128)(2,1)}) custom-call(s32[8,256]{1,0:T(8,128)} %bitcast.2, s32[8,256]{1,0:T(8,128)} %bitcast.3, bf16[1,512,512]{2,1,0:T(8,128)(2,1)} %x_hbm.1, bf16[1,512,512]{2,1,0:T(8,128)(2,1)} %c_hbm.1, bf16[512,1536]{1,0:T(8,128)(2,1)} %w_hbm.1, bf16[512,512]{1,0:T(8,128)(2,1)} %wo_hbm.1), custom_call_target="tpu_custom_call" | custom-call | flops 8000000000 | bytes 8388608 | tf_op jit(solution)/shard_map/layer/pallas_call | solution.py:588
  77.9 3.4 %finish.1 = (f32[512,1536]{1,0:T(8,128)}, f32[512,512]{1,0:T(8,128)}, bf16[1,512,512]{2,1,0:T(8,128)(2,1)}) custom-call(bf16[4,512,512]{2,1,0:T(8,128)(2,1)} %get-tuple-element.8.chunks, bf16[1,512,512]{2,1,0:T(8,128)(2,1)} %get-tuple-element.9.features), custom_call_target="tpu_custom_call" | custom-call | tf_op jit(solution)/shard_map/finish/pallas_call | solution.py:650
